TPU v7x, 32 devices: a whole 2x2x4 slice. The times are simulated.
32 devices in a mesh: dp: 8 (over y, x, core), rows: 4 (over z).
Axes of the slice: x: 2, y: 2, z: 4, core: 2. Of those that a mesh axis runs over, the one named last changes fastest.
Arguments:
- tokens: bfloat16 [32, 28, 70, 384], P('dp', 'rows'), may hold values from -6 to 6
- heights: int32 [32], P('dp'), may hold values from 1 to 4, as said below
- conv_weight: bfloat16 [4, 3, 3, 384], replicated, may hold values from -2 to 2
- conv_bias: bfloat16 [4, 384], replicated, may hold values from -1.5 to 1.5
- norm_gain: bfloat16 [4, 384], replicated, may hold values from 0.5 to 1.5
- norm_shift: bfloat16 [4, 384], replicated, may hold values from -1 to 1
- mix_weight: bfloat16 [2, 384, 1152], replicated, may hold values from -0.3125 to 0.3125
- window_bias: bfloat16 [768], replicated, may hold values from -1.5 to 1.5
- channel_bias: bfloat16 [1152], replicated, may hold values from -0.5 to 0.5
- out_weight: bfloat16 [2, 384, 384], replicated, may hold values from -0.875 to 0.875
- out_bias: bfloat16 [2, 384], replicated, may hold values from -1.5 to 1.5
- up_weight: bfloat16 [2, 384, 1536], replicated, may hold values from -0.3125 to 0.3125
- up_bias: bfloat16 [2, 1536], replicated, may hold values from -1.5 to 1.5
- down_weight: bfloat16 [2, 1536, 384], replicated, may hold values from -0.15625 to 0.15625
- down_bias: bfloat16 [2, 384], replicated, may hold values from -1.5 to 1.5
- cotangent: bfloat16 [32, 28, 70, 384], P('dp', 'rows'), may hold values from -6 to 6
Outputs:
- result: bfloat16 [32, 28, 70, 384], P('dp', 'rows')
- tokens_grad: float32 [32, 28, 70, 384], P('dp', 'rows')
- conv_weight_grad: float32 [4, 3, 3, 384], replicated
- conv_bias_grad: float32 [4, 384], replicated
- norm_gain_grad: float32 [4, 384], replicated
- norm_shift_grad: float32 [3, 384], replicated
- final_shift_grad: float32 [384], replicated
- mix_weight_grad: float32 [2, 384, 1152], replicated
- window_bias_grad: float32 [768], replicated
- channel_bias_grad: float32 [1152], replicated
- out_weight_grad: float32 [2, 384, 384], replicated
- out_bias_grad: float32 [2, 384], replicated
- up_weight_grad: float32 [2, 384, 1536], replicated
- up_bias_grad: float32 [2, 1536], replicated
- down_weight_grad: float32 [2, 1536, 384], replicated
- down_bias_grad: float32 [2, 384], replicated
Inputs may be any that keep to these rules, and one draw needn't show every extreme that they name: `heights`: in each block of 4 images of one index of dp, one image is 4 window rows tall.
All inputs are finite; a program needn't handle non-finite values.
Results may differ from a plain program's by a relative error of at most 0.019.
Values may be sent and summed in bfloat16 or wider, within the bound.
No kernel may reach another device: no remote copies, remote signals or barrier semaphores. Data moves between devices by JAX's collectives and lax.ppermute only.
A program may use at most 320 MiB of HBM per device.

v0:
```python
import functools

import jax
import jax.numpy as jnp
import numpy as np
from jax import lax
from jax.experimental import pallas as pl
from jax.experimental.pallas import tpu as pltpu
from jax.sharding import Mesh
from jax.sharding import PartitionSpec as P

HEADS = 12
HEAD_DIM = 32
EPS = 1e-05
WIN = 7
SLOT = 64
LANES = 128
F32 = jnp.float32
BF16 = jnp.bfloat16
SCALE = HEAD_DIM ** (-0.5)
LOG2E = 1.4426950408889634
ROOT_HALF = 0.7071067811865476
VMEM_LIMIT = 58 * 1024 * 1024
SMALL_ROWS = 512


def dot(left, right):
    return jnp.dot(left, right, preferred_element_type=F32)


def dot_nt(left, right):
    return lax.dot_general(left, right, (((1,), (1,)), ((), ())), preferred_element_type=F32)


def dot_tn(left, right):
    return lax.dot_general(left, right, (((0,), (0,)), ((), ())), preferred_element_type=F32)


def low(value):
    return value.astype(BF16).astype(F32)


def fold(value):
    rows, cols = value.shape
    return jnp.sum(value.reshape(rows // 8, 8, cols), axis=0)


def loop(count, step, body):
    for at in range(0, count, step):
        body(at)


def lane_tiles(chans):
    return [slice(t, t + LANES) for t in range(0, chans, LANES)]


def gelu_parts(value):
    size = jnp.abs(value)
    t = 1.0 / (1.0 + (0.3275911 * ROOT_HALF) * size)
    poly = t * (
        0.127414796
        + t * (-0.142248368 + t * (0.7107068705 + t * (-0.7265760135 + t * 0.5307027145)))
    )
    bell = jnp.exp2(value * value * (-0.5 * LOG2E))
    tail = poly * bell
    cdf = jnp.where(value >= 0.0, 1.0 - tail, tail)
    return value * cdf, cdf + value * bell * 0.3989422804014327


def norm_of(value, gain, shift):
    centre = value - jnp.mean(value, axis=-1, keepdims=True)
    spread = jnp.mean(centre * centre, axis=-1, keepdims=True)
    return centre * lax.rsqrt(spread + EPS) * gain + shift


def norm_back(value, gain, normed_grad):
    centre = value - jnp.mean(value, axis=-1, keepdims=True)
    inv = lax.rsqrt(jnp.mean(centre * centre, axis=-1, keepdims=True) + EPS)
    unit = centre * inv
    unit_grad = normed_grad * gain
    first = jnp.mean(unit_grad, axis=-1, keepdims=True)
    second = jnp.mean(unit_grad * unit, axis=-1, keepdims=True)
    return inv * (unit_grad - first - unit * second), normed_grad * unit


def fill_source(src, main, prev, after, halo, step, steps, width):
    rows = main.shape[0]
    src[pl.ds(0, width), :] = jnp.where(step == 0, halo[0:width, :], low(prev[...]))
    src[pl.ds(rows + width, width), :] = jnp.where(
        step == steps - 1, halo[width : 2 * width, :], low(after[...])
    )

    def body(at):
        src[pl.ds(at + width, 2 * width), :] = low(main[pl.ds(at, 2 * width), :])

    loop(rows // (2 * width) * 2 * width, 2 * width, body)
    if rows % (2 * width):
        at = rows - width
        src[pl.ds(at + width, width), :] = low(main[pl.ds(at, width), :])


def conv_tile(src, vec, at, tile, width, lanes, flipped):
    rows = [src[pl.ds(at + width * d, tile), lanes] for d in range(3)]
    sums = []
    for col in range(3):
        total = None
        for row in range(3):
            k = (2 - row) * 3 + (2 - col) if flipped else row * 3 + col
            term = rows[row] * vec[k : k + 1, lanes]
            total = term if total is None else total + term
        sums.append(total)
    return sums[1] + pltpu.roll(sums[0], 1, 0) + pltpu.roll(sums[2], tile - 1, 0), rows


def conv_weight_tile(acc, rows, field, tile, lanes):
    shifted = [pltpu.roll(field, 1, 0), field, pltpu.roll(field, tile - 1, 0)]
    for row in range(3):
        for col in range(3):
            k = row * 3 + col
            acc[8 * k : 8 * k + 8, lanes] += fold(shifted[col] * rows[2 - row])


def block_heads(part):
    lane = lax.broadcasted_iota(jnp.int32, part.shape, 1)
    zero = jnp.zeros_like(part)
    return jnp.concatenate(
        [jnp.where(lane // HEAD_DIM == h, part, zero) for h in range(LANES // HEAD_DIM)], axis=0
    )


def window_forward_kernel(
    tok, prev, after, halo, mask, vec, mix, mix_b, out_w, gather, x1, nw, mw, ow, x2, src, keep, probs
):
    step, steps = pl.program_id(0), pl.num_programs(0)
    rows, width, chans = tok.shape
    src[pl.ds(0, width), :] = jnp.where(step == 0, halo[0:width, :], prev[0].astype(F32))
    src[pl.ds((rows + 1) * width, width), :] = jnp.where(
        step == steps - 1, halo[width : 2 * width, :], after[0].astype(F32)
    )
    for i in range(rows):
        src[pl.ds((i + 1) * width, width), :] = tok[i].astype(F32)

    def conv_body(at):
        region = mask[pl.ds(at, width), :]
        for lanes in lane_tiles(chans):
            got, near = conv_tile(src, vec, at, width, width, lanes, False)
            x1[pl.ds(at, width), lanes] = region * (near[1] + got + vec[9:10, lanes])

    loop(rows * width, width, conv_body)

    normed = norm_of(x1[...], vec[10:11, :], vec[11:12, :]).astype(BF16)
    normed = dot(gather[...], normed).astype(BF16)
    nw[...] = normed
    mw[...] = (dot(normed, mix[...]) + mix_b[...]).astype(BF16)
    windows = nw.shape[0] // SLOT
    lane = lax.broadcasted_iota(jnp.int32, (SLOT, LANES), 1)
    left = lane < SLOT
    real = lane % SLOT < WIN * WIN
    ones = (
        lax.broadcasted_iota(jnp.int32, (4 * SLOT, LANES), 0) // SLOT
        == lax.broadcasted_iota(jnp.int32, (4 * SLOT, LANES), 1) // HEAD_DIM
    ).astype(BF16)
    floor = -1e30

    places = [(at, lanes) for at in range(0, windows * SLOT, SLOT) for lanes in lane_tiles(chans)]
    for n, (at, lanes) in enumerate(places):
        query = mw[at : at + SLOT, lanes]
        key = mw[at : at + SLOT, chans + lanes.start : chans + lanes.stop]
        scores = dot_nt(query, block_heads(key))
        for half in range(2):
            part = jnp.where(real, scores[:, half * LANES : (half + 1) * LANES], floor)
            top_l = jnp.max(jnp.where(left, part, floor), axis=1, keepdims=True)
            top_r = jnp.max(jnp.where(left, floor, part), axis=1, keepdims=True)
            top = jnp.where(left, top_l, top_r)
            raised = jnp.exp2((part - top) * (SCALE * LOG2E)).astype(BF16)
            probs[n * SLOT : (n + 1) * SLOT, half * LANES : (half + 1) * LANES] = raised
    for n, (at, lanes) in enumerate(places):
        value = mw[at : at + SLOT, 2 * chans + lanes.start : 2 * chans + lanes.stop]
        both = dot(
            probs[n * SLOT : (n + 1) * SLOT, :], jnp.concatenate([block_heads(value), ones], axis=1)
        )
        ow[at : at + SLOT, lanes] = (both[:, :LANES] / both[:, LANES:]).astype(BF16)
    merged = dot_tn(gather[...], ow[...]).astype(BF16)
    keep[...] = dot(merged, out_w[...])

    def out_body(at):
        region = mask[pl.ds(at, width), :]
        for lanes in lane_tiles(chans):
            x2[pl.ds(at, width), lanes] = region * (
                x1[pl.ds(at, width), lanes] + keep[pl.ds(at, width), lanes] + vec[12:13, lanes]
            )

    loop(rows * width, width, out_body)


def conv_forward(main, prev, after, halo, mask, vec, out, src, width):
    step, steps = pl.program_id(0), pl.num_programs(0)
    rows, chans = main.shape
    fill_source(src, main, prev, after, halo, step, steps, width)
    tile = 2 * width

    def body(at):
        region = mask[pl.ds(at, tile), :]
        for lanes in lane_tiles(chans):
            got, _ = conv_tile(src, vec, at, tile, width, lanes, False)
            out[pl.ds(at, tile), lanes] = region * (
                main[pl.ds(at, tile), lanes] + got + vec[9:10, lanes]
            )

    loop(rows, tile, body)


def norm_forward(value, vec, out):
    out[...] = norm_of(value[...], vec[10:11, :], vec[11:12, :]).astype(BF16)


def mlp_body(normed, up_w, up_b, down_w, hidden, slope, keep):
    rows = normed.shape[0]
    for at in range(0, up_w.shape[1], 256):
        cols = slice(at, at + 256)
        pre = dot(normed[...], up_w[:, cols]) + up_b[:, cols]
        for row in range(0, rows, 144):
            act, der = gelu_parts(pre[row : row + 144])
            hidden[row : row + 144, cols] = act.astype(BF16)
            slope[row : row + 144, cols] = der.astype(BF16)
        part = dot(hidden[:, cols], down_w[cols, :])
        if at == 0:
            keep[...] = part
        else:
            keep[...] += part


def add_residual(state, branch, mask, vec, out):
    chans = state.shape[1]

    def body(at):
        region = mask[pl.ds(at, 144), :]
        for lanes in lane_tiles(chans):
            out[pl.ds(at, 144), lanes] = (
                region
                * (state[pl.ds(at, 144), lanes] + branch[pl.ds(at, 144), lanes] + vec[12:13, lanes])
            ).astype(out.dtype)

    loop(state.shape[0], 144, body)


def mlp_forward_kernel(
    main, prev, after, halo, mask, vec, up_w, up_b, down_w, x3, x4, normed, hidden, slope, src, keep
):
    width = prev.shape[0]
    conv_forward(main, prev, after, halo, mask, vec, x3, src, width)
    norm_forward(x3, vec, normed)
    mlp_body(normed, up_w, up_b, down_w, hidden, slope, keep)
    add_residual(x3, keep, mask, vec, x4)


def norm_backward(state, normed_grad, grad, vec, small, out, gain_row):
    part = normed_grad[...]
    back, scaled = norm_back(state[...], vec[10:11, :], part)
    out[...] = grad[...].astype(F32) + back
    small[gain_row : gain_row + 8, :] += fold(scaled)
    small[gain_row + 8 : gain_row + 16, :] += fold(part)


def mlp_down_back(rounded, normed, hidden, slope, pre_grad, up_w, down_w, up_g, up_bg, down_g):
    rows = rounded.shape[0]
    for at in range(0, up_w.shape[1], 256):
        cols = slice(at, at + 256)
        hidden_grad = dot_nt(rounded[...], down_w[cols, :])
        total = None
        for row in range(0, rows, 144):
            part = hidden_grad[row : row + 144] * slope[row : row + 144, cols].astype(F32)
            pre_grad[row : row + 144, cols] = part.astype(BF16)
            total = fold(part) if total is None else total + fold(part)
        up_bg[:, cols] += total
        up_g[:, cols] += dot_tn(normed[...], pre_grad[:, cols])
        down_g[cols, :] += dot_tn(hidden[:, cols], rounded[...])


def mlp_both(normed, cot, up_w, up_b, down_w, hidden, pre_grad, up_g, up_bg, down_g):
    rows = normed.shape[0]

    def block(at):
        cols = pl.ds(pl.multiple_of(at, 256), 256)
        pre = dot(normed[...], up_w[:, cols]) + up_b[:, cols]
        hidden_grad = dot_nt(cot[...], down_w[cols, :])
        total = None
        for row in range(0, rows, 144):
            act, der = gelu_parts(pre[row : row + 144])
            hidden[row : row + 144, cols] = act.astype(BF16)
            part = hidden_grad[row : row + 144] * der
            pre_grad[row : row + 144, cols] = part.astype(BF16)
            total = fold(part) if total is None else total + fold(part)
        up_bg[:, cols] += total
        up_g[:, cols] += dot_tn(normed[...], pre_grad[:, cols])
        down_g[cols, :] += dot_tn(hidden[:, cols], cot[...])

    def pair(i, carry):
        block(i * 512)
        block(i * 512 + 256)
        return carry

    lax.fori_loop(0, up_w.shape[1] // 512, pair, 0)


def column_blocks(source, chans):
    return [source.at[:, col : col + chans] for col in range(0, source.shape[1], chans)]


def spread(core, kept, sent, blocks):
    half = kept.shape[0]
    for flag in range(2):

        @pl.when(core[0] == flag)
        def _():
            at = 0
            for block in blocks:
                rows = block.shape[0]
                cuts = [0, rows] if not at < half < at + rows else [0, half - at, rows]
                for low_cut, high_cut in zip(cuts, cuts[1:]):
                    start = at + low_cut
                    target = kept if (start >= half) == (flag == 1) else sent
                    start = start % half
                    target[start : start + high_cut - low_cut, :] = block[
                        low_cut:high_cut, :
                    ].astype(BF16)
                at += rows


def last_step():
    return pl.program_id(0) == pl.num_programs(0) - 1


def zero_first(*refs):
    @pl.when(pl.program_id(0) == 0)
    def _():
        for ref in refs:
            ref[...] = jnp.zeros_like(ref)


def last_mlp_kernel(
    main, prev, after, halo, mask, vec, up_w, up_b, down_w, cot,
    result, grad, packed, up_bg, small,
    src, x7, keep, back, normed, hidden, pre_grad, up_g, down_g,
):
    width = prev.shape[0]
    zero_first(up_g, up_bg, down_g, small)
    conv_forward(main, prev, after, halo, mask, vec, x7, src, width)
    norm_forward(x7, vec, normed)
    mlp_both(normed, cot, up_w, up_b, down_w, hidden, pre_grad, up_g, up_bg, down_g)
    keep[...] = dot(hidden[...], down_w[...])
    back[...] = dot_nt(pre_grad[...], up_w[...])
    add_residual(x7, keep, mask, vec, result)
    small[0:8, :] += fold(cot[...].astype(F32))
    norm_backward(x7, back, cot, vec, small, grad, 8)

    @pl.when(last_step())
    def _():
        at = 0
        for block in column_blocks(up_g, packed.shape[1]) + [down_g]:
            packed[at : at + block.shape[0], :] = block[...].astype(BF16)
            at += block.shape[0]


def conv_backward(main, prev, after, halo, mask, vec, field, out, conv_g, small, src, width):
    step, steps = pl.program_id(0), pl.num_programs(0)
    rows, chans = main.shape
    fill_source(src, main, prev, after, halo, step, steps, width)
    tile = 72

    def body(at):
        region = mask[pl.ds(at, tile), :]
        for lanes in lane_tiles(chans):
            got, near = conv_tile(src, vec, at, tile, width, lanes, True)
            grad = main[pl.ds(at, tile), lanes]
            out[pl.ds(at, tile), lanes] = (region * (grad + got)).astype(out.dtype)
            conv_weight_tile(conv_g, near, low(field[pl.ds(at, tile), lanes]), tile, lanes)
            small[0:8, lanes] += fold(grad)

    loop(rows, tile, body)


def fold_rows(source, small, row):
    def body(at):
        small[row : row + 8, :] += fold(source[pl.ds(at, 72), :])

    loop(source.shape[0], 72, body)


def channel_mix_kernel(
    main, prev, after, halo, mask, vec, mix, mix_b, x5, normed, mixed, gram, src
):
    width = prev.shape[0]
    chans = main.shape[1]
    zero_first(gram)
    conv_forward(main, prev, after, halo, mask, vec, x5, src, width)
    norm_forward(x5, vec, normed)
    rows = main.shape[0]
    for part in range(3):
        cols = slice(part * chans, (part + 1) * chans)
        got = dot(normed[...], mix[:, cols]) + mix_b[:, cols]
        if part == 1:
            got = got * jnp.concatenate([mask[...]] * (chans // LANES), axis=1)
        mixed[:, cols] = got.astype(BF16)
    for t, lanes in enumerate(lane_tiles(chans)):
        gram[t] += dot_tn(
            mixed[:, chans + lanes.start : chans + lanes.stop],
            mixed[:, 2 * chans + lanes.start : 2 * chans + lanes.stop],
        )


def same_head():
    row = lax.broadcasted_iota(jnp.int32, (LANES, LANES), 0)
    col = lax.broadcasted_iota(jnp.int32, (LANES, LANES), 1)
    return row // HEAD_DIM == col // HEAD_DIM


def channel_weights(gram, scale):
    own = same_head()
    logits = jnp.where(own, gram * scale, -1e30)
    top = jnp.max(logits, axis=1, keepdims=True)
    raised = jnp.where(own, jnp.exp(logits - top), 0.0)
    return raised / jnp.sum(raised, axis=1, keepdims=True)


def channel_out_kernel(mixed, gram, scale, x5, mask, vec, out_w, o2, x6, keep):
    chans = x5.shape[1]
    for t, lanes in enumerate(lane_tiles(chans)):
        weights = channel_weights(gram[t], scale[0:1, :]).astype(BF16)
        o2[:, lanes] = dot_nt(mixed[:, lanes], weights).astype(BF16)
    keep[...] = dot(o2[...], out_w[...])
    add_residual(x5, keep, mask, vec, x6)


def channel_grad_kernel(
    main, prev, after, halo, mask, vec, x6, mixed, o2, out_w,
    grad, attended_grad, weights_g, packed, conv_g, small, src, rounded, out_g,
):
    width = prev.shape[0]
    chans = main.shape[1]
    zero_first(weights_g, out_g, conv_g, small)
    conv_backward(main, prev, after, halo, mask, vec, x6, grad, conv_g, small, src, width)
    rounded[...] = grad[...].astype(BF16)
    fold_rows(grad, small, 8)
    out_g[...] += dot_tn(o2[...], rounded[...])
    attended_grad[...] = dot_nt(rounded[...], out_w[...]).astype(BF16)
    for t, lanes in enumerate(lane_tiles(chans)):
        weights_g[t] += dot_tn(attended_grad[:, lanes], mixed[:, lanes])

    @pl.when(last_step())
    def _():
        packed[...] = out_g[...].astype(BF16)


def channel_back_kernel(
    attended_grad, mixed, gram, weights_g, scale, normed, x5, g6, mask, vec, mix,
    grad, packed, mix_bg, small, mixed_grad, keep, mix_g,
):
    chans = x5.shape[1]
    zero_first(mix_g, mix_bg, small)
    own = same_head()
    wide = mask[...]
    for t, lanes in enumerate(lane_tiles(chans)):
        weights = channel_weights(gram[t], scale[0:1, :])
        back = jnp.where(own, weights_g[t], 0.0)
        logit = weights * (back - jnp.sum(back * weights, axis=1, keepdims=True))
        logit = logit.astype(BF16)
        key = slice(chans + lanes.start, chans + lanes.stop)
        val = slice(2 * chans + lanes.start, 2 * chans + lanes.stop)
        query_grad = dot(attended_grad[:, lanes], weights.astype(BF16))
        key_grad = dot_nt(mixed[:, val], logit) * scale[0:1, :] * wide
        value_grad = dot(mixed[:, key], logit) * scale[0:1, :]
        for cols, part in ((lanes, query_grad), (key, key_grad), (val, value_grad)):
            mix_bg[:, cols] += fold(part)
            mixed_grad[:, cols] = part.astype(BF16)
    for part in range(3):
        cols = slice(part * chans, (part + 1) * chans)
        mix_g[part * chans : (part + 1) * chans, :] += dot_tn(normed[...], mixed_grad[:, cols])
    keep[...] = dot_nt(mixed_grad[...], mix[...])
    norm_backward(x5, keep, g6, vec, small, grad, 0)

    @pl.when(last_step())
    def _():
        packed[...] = mix_g[...].astype(BF16)


def mlp_back_kernel(
    main, prev, after, halo, mask, vec_conv, vec, x4, x3, normed, hidden, slope, up_w, down_w, mlp1, mix1, out1, core,
    grad, kept, sent, up_bg, conv_g, small,
    src, g4, rounded, keep, pre_grad, up_g, down_g,
):
    width = prev.shape[0]
    zero_first(up_g, up_bg, down_g, conv_g, small)
    conv_backward(main, prev, after, halo, mask, vec_conv, x4, g4, conv_g, small, src, width)
    rounded[...] = g4[...].astype(BF16)
    fold_rows(g4, small, 8)
    mlp_down_back(rounded, normed, hidden, slope, pre_grad, up_w, down_w, up_g, up_bg, down_g)
    keep[...] = dot_nt(pre_grad[...], up_w[...])
    norm_backward(x3, keep, g4, vec, small, grad, 16)

    @pl.when(last_step())
    def _():
        spread(core, kept, sent, [mlp1, mix1, out1] + column_blocks(up_g, kept.shape[1]) + [down_g])


def window_back_kernel(
    main, prev, after, halo, mask, vec_conv, vec, x2, x1, nw, mw, ow, mix, out_w, gather,
    grad, packed, mix_bg, conv_g, small,
    src, mix_g, out_g, g2, gw, dow, dmw, keep, probs, slopes,
):
    width = prev.shape[0]
    chans = main.shape[1]
    zero_first(mix_g, mix_bg, out_g, conv_g, small)
    conv_backward(main, prev, after, halo, mask, vec_conv, x2, g2, conv_g, small, src, width)
    fold_rows(g2, small, 8)
    gw[...] = dot(gather[...], g2[...].astype(BF16)).astype(BF16)
    out_g[...] += dot_tn(ow[...], gw[...])
    dow[...] = dot_nt(gw[...], out_w[...]).astype(BF16)
    windows = nw.shape[0] // SLOT
    real = lax.broadcasted_iota(jnp.int32, (SLOT, 4 * SLOT), 0) < WIN * WIN
    head = lax.broadcasted_iota(jnp.int32, (SLOT, LANES), 1) // HEAD_DIM

    places = [(at, lanes) for at in range(0, windows * SLOT, SLOT) for lanes in lane_tiles(chans)]
    for n, (at, lanes) in enumerate(places):
        rows = slice(at, at + SLOT)
        query = mw[rows, lanes]
        key = mw[rows, chans + lanes.start : chans + lanes.stop]
        value = mw[rows, 2 * chans + lanes.start : 2 * chans + lanes.stop]
        scores = jnp.where(real, dot_nt(key, block_heads(query)), -1e30)
        top = jnp.max(scores, axis=0, keepdims=True)
        raised = jnp.exp2((scores - top) * (SCALE * LOG2E))
        share = raised * (1.0 / jnp.sum(raised, axis=0, keepdims=True))
        share_grad = dot_nt(value, block_heads(dow[rows, lanes]))
        inner = jnp.sum(share_grad * share, axis=0, keepdims=True)
        probs[n * SLOT : (n + 1) * SLOT, :] = share.astype(BF16)
        slopes[n * SLOT : (n + 1) * SLOT, :] = (share * (share_grad - inner)).astype(BF16)
    for n, (at, lanes) in enumerate(places):
        rows = slice(at, at + SLOT)
        key_cols = slice(chans + lanes.start, chans + lanes.stop)
        value_cols = slice(2 * chans + lanes.start, 2 * chans + lanes.stop)
        share, slope = probs[n * SLOT : (n + 1) * SLOT, :], slopes[n * SLOT : (n + 1) * SLOT, :]
        value_grad = dot(share, block_heads(dow[rows, lanes]))
        key_grad = dot(slope, block_heads(mw[rows, lanes])) * SCALE
        full = dot_tn(slope, mw[rows, key_cols])
        query_grad = jnp.zeros((SLOT, LANES), F32)
        for h in range(LANES // HEAD_DIM):
            query_grad = jnp.where(head == h, full[h * SLOT : (h + 1) * SLOT], query_grad)
        query_grad = query_grad * SCALE
        for cols, part in ((lanes, query_grad), (key_cols, key_grad), (value_cols, value_grad)):
            dmw[rows, cols] = part.astype(BF16)
            mix_bg[:, cols] += fold(part)
    for part in range(3):
        cols = slice(part * chans, (part + 1) * chans)
        mix_g[part * chans : (part + 1) * chans, :] += dot_tn(nw[...], dmw[:, cols])
    normed_grad = dot_nt(dmw[...], mix[...]).astype(BF16)
    keep[...] = dot_tn(gather[...], normed_grad)
    norm_backward(x1, keep, g2, vec, small, grad, 16)

    @pl.when(last_step())
    def _():
        packed[: 3 * chans, :] = mix_g[...].astype(BF16)
        packed[3 * chans :, :] = out_g[...].astype(BF16)


def token_grad_kernel(main, prev, after, halo, mask, vec, field, core, win0, *refs):
    parts, (out, kept, sent, src, conv_g, small, rows) = refs[:-7], refs[-7:]
    width = prev.shape[0]
    zero_first(conv_g, small)
    conv_backward(main, prev, after, halo, mask, vec, field, out, conv_g, small, src, width)

    @pl.when(last_step())
    def _():
        small_sums(core, win0, conv_g, *parts[:3], small, *parts[3:], kept, sent, rows)


def call(kernel, steps, ins, outs, scratch, cost, after=()):
    count = len(ins)

    def body(*refs):
        kernel(*refs[:count], *refs[count + len(after) :])

    def spec(block, index):
        if block is None:
            return pl.BlockSpec(memory_space=pltpu.SMEM)
        if isinstance(index, int):
            fixed = (index,) + tuple(0 for _ in block[1:])
            return pl.BlockSpec((None,) + block[1:], lambda i: fixed, pipeline_mode=pl.Buffered(1))
        fixed = tuple(0 for _ in block)
        if index is None:
            return pl.BlockSpec(block, lambda i: fixed, pipeline_mode=pl.Buffered(1))
        return pl.BlockSpec(block, index)

    def out_spec(block, index):
        fixed = tuple(0 for _ in block)
        return pl.BlockSpec(block, (lambda i: fixed) if index is None else index)

    return pl.pallas_call(
        body,
        grid=(steps,),
        in_specs=[spec(block, index) for _, block, index in ins]
        + [pl.BlockSpec(memory_space=pl.ANY) for _ in after],
        out_specs=[out_spec(block, index) for _, _, block, index in outs],
        out_shape=[jax.ShapeDtypeStruct(shape, dtype) for shape, dtype, _, _ in outs],
        scratch_shapes=[pltpu.VMEM(shape, dtype) for shape, dtype in scratch],
        compiler_params=pltpu.CompilerParams(vmem_limit_bytes=VMEM_LIMIT),
        cost_estimate=pl.CostEstimate(flops=1, bytes_accessed=cost * 3_600_000, transcendentals=0),
    )(*[array for array, _, _ in ins], *after)


def gather_matrix(cols, width):
    windows = cols // WIN
    slot = np.arange(windows * SLOT)[:, None]
    window, inside = slot // SLOT, slot % SLOT
    source = inside // WIN * width + window * WIN + inside % WIN
    patch = np.arange(WIN * width)[None, :]
    return jnp.asarray(((source == patch) & (inside < WIN * WIN)).astype(BF16))


def prepare_kernel(conv_w, conv_b, gain, shift, out_b, down_b, up_b, vecs, up_bias):
    for k in range(4):
        for i in range(3):
            vecs[k, 3 * i : 3 * i + 3, :] = conv_w[k, i].astype(F32)
        last = out_b if k % 2 == 0 else down_b
        for at, ref, row in ((9, conv_b, k), (10, gain, k), (11, shift, k), (12, last, k // 2)):
            vecs[k, at : at + 1, :] = ref[row : row + 1, :].astype(F32)
    for k in range(2):
        up_bias[k] = up_b[k : k + 1, :].astype(F32)


def prepare(*parts):
    chans, ff = parts[0].shape[-1], parts[-1].shape[-1]
    return pl.pallas_call(
        prepare_kernel,
        out_shape=tuple(jax.ShapeDtypeStruct(x, F32) for x in ((4, 16, chans), (2, 1, ff))),
    )(*parts)


def image_block(x0, cot, tok_halo, mask, scale, halo_of, across, weights, small, cols, core, send_result, share_cores, share_planes):
    mix_w, out_w, up_w, down_w = weights
    height, width, chans = x0.shape
    tokens = height * width
    ff = up_w.shape[2]
    vecs, up_bias, bias0, bias1 = small
    gather = gather_matrix(cols, width)
    wrows = cols // WIN * SLOT
    unit = WIN * width
    units = height // WIN
    chunk = 2 * unit if units % 2 == 0 else unit
    chunks = tokens // chunk

    def near(array, rows):
        per = rows // width
        return [
            (array, (rows, chans), lambda i: (i, 0)),
            (array, (width, chans), lambda i: (jnp.maximum(i * per - 1, 0), 0)),
            (array, (width, chans), lambda i: (jnp.minimum(i * per + per, height - 1), 0)),
            (halo_of(array), (2 * width, chans), None),
        ]

    def rows_in(array, rows):
        return (array, (rows, array.shape[1]), lambda i: (i, 0))

    def whole(array):
        return (array, array.shape, None)

    def layer(array, k):
        return (array, array.shape, k)

    def rows_out(cols_, dtype, rows=chunk, total=tokens):
        return ((total, cols_), dtype, (rows, cols_), lambda i: (i, 0))

    def sums(*shape, dtype=F32):
        return (shape, dtype, shape, None)

    def vec(k):
        return layer(vecs, k)

    scalar = (core, None, None)

    x1, nw, mw, ow, x2 = call(
        window_forward_kernel,
        units,
        [
            (x0, (WIN, width, chans), lambda i: (i, 0, 0)),
            (x0, (1, width, chans), lambda i: (jnp.maximum(i * WIN - 1, 0), 0, 0)),
            (x0, (1, width, chans), lambda i: (jnp.minimum(i * WIN + WIN, height - 1), 0, 0)),
            whole(tok_halo),
            rows_in(mask, unit),
            vec(0),
            layer(mix_w, 0),
            whole(bias0),
            layer(out_w, 0),
            whole(gather),
        ],
        [
            rows_out(chans, F32, unit),
            rows_out(chans, BF16, wrows, units * wrows),
            rows_out(3 * chans, BF16, wrows, units * wrows),
            rows_out(chans, BF16, wrows, units * wrows),
            rows_out(chans, F32, unit),
        ],
        [
            ((unit + 2 * width, chans), F32),
            ((unit, chans), F32),
            ((wrows * chans // LANES, 4 * SLOT), BF16),
        ],
        20,
    )
    x3, x4, n1, h1, s1 = call(
        mlp_forward_kernel,
        chunks,
        near(x2, chunk) + [rows_in(mask, chunk), vec(1), layer(up_w, 0), layer(up_bias, 0), layer(down_w, 0)],
        [
            rows_out(chans, F32),
            rows_out(chans, F32),
            rows_out(chans, BF16),
            rows_out(ff, BF16),
            rows_out(ff, BF16),
        ],
        [((chunk + 2 * width, chans), F32), ((chunk, chans), F32)],
        25,
    )
    x5, n2, m2, gram = call(
        channel_mix_kernel,
        chunks,
        near(x4, chunk) + [rows_in(mask, chunk), vec(2), layer(mix_w, 1), whole(bias1)],
        [
            rows_out(chans, F32),
            rows_out(chans, BF16),
            rows_out(3 * chans, BF16),
            sums(chans // LANES, LANES, LANES),
        ],
        [((chunk + 2 * width, chans), F32)],
        11,
    )
    gram = across(gram)
    o2, x6 = call(
        channel_out_kernel,
        chunks,
        [
            rows_in(m2, chunk),
            whole(gram),
            whole(scale),
            rows_in(x5, chunk),
            rows_in(mask, chunk),
            vec(2),
            layer(out_w, 1),
        ],
        [rows_out(chans, BF16), rows_out(chans, F32)],
        [((chunk, chans), F32)],
        7,
    )
    result, g7, mlp1, up_bg1, small7 = call(
        last_mlp_kernel,
        chunks,
        near(x6, chunk)
        + [
            rows_in(mask, chunk),
            vec(3),
            layer(up_w, 1),
            layer(up_bias, 1),
            layer(down_w, 1),
            rows_in(cot, chunk),
        ],
        [
            rows_out(chans, BF16),
            rows_out(chans, F32),
            sums(2 * ff, chans, dtype=BF16),
            sums(8, ff),
            sums(24, chans),
        ],
        [
            ((chunk + 2 * width, chans), F32),
            ((chunk, chans), F32),
            ((chunk, chans), F32),
            ((chunk, chans), F32),
            ((chunk, chans), BF16),
            ((chunk, ff), BF16),
            ((chunk, ff), BF16),
            ((chans, ff), F32),
            ((ff, chans), F32),
        ],
        38,
    )
    result = send_result(result)
    g6, do2, weights_g, out1, conv_g3, small6 = call(
        channel_grad_kernel,
        chunks,
        near(g7, chunk)
        + [
            rows_in(mask, chunk),
            vec(3),
            rows_in(x6, chunk),
            (m2, (chunk, chans), lambda i: (i, 0)),
            rows_in(o2, chunk),
            layer(out_w, 1),
        ],
        [
            rows_out(chans, F32),
            rows_out(chans, BF16),
            sums(chans // LANES, LANES, LANES),
            sums(chans, chans, dtype=BF16),
            sums(72, chans),
            sums(16, chans),
        ],
        [((chunk + 2 * width, chans), F32), ((chunk, chans), BF16), ((chans, chans), F32)],
        13,
    )
    weights_g = across(weights_g)
    g5, mix1, mix_bg1, small5 = call(
        channel_back_kernel,
        chunks,
        [
            rows_in(do2, chunk),
            rows_in(m2, chunk),
            whole(gram),
            whole(weights_g),
            whole(scale),
            rows_in(n2, chunk),
            rows_in(x5, chunk),
            rows_in(g6, chunk),
            rows_in(mask, chunk),
            vec(2),
            layer(mix_w, 1),
        ],
        [
            rows_out(chans, F32),
            sums(3 * chans, chans, dtype=BF16),
            sums(8, 3 * chans),
            sums(16, chans),
        ],
        [((chunk, 3 * chans), BF16), ((chunk, chans), F32), ((3 * chans, chans), F32)],
        16,
    )
    g3, kept0, sent0, up_bg0, conv_g2, small3 = call(
        mlp_back_kernel,
        chunks,
        near(g5, chunk)
        + [
            rows_in(mask, chunk),
            vec(2),
            vec(1),
            rows_in(x4, chunk),
            rows_in(x3, chunk),
            rows_in(n1, chunk),
            rows_in(h1, chunk),
            rows_in(s1, chunk),
            layer(up_w, 0),
            layer(down_w, 0),
            whole(mlp1),
            whole(mix1),
            whole(out1),
            scalar,
        ],
        [
            rows_out(chans, F32),
            sums(2 * ff + 2 * chans, chans, dtype=BF16),
            sums(2 * ff + 2 * chans, chans, dtype=BF16),
            sums(8, ff),
            sums(72, chans),
            sums(32, chans),
        ],
        [
            ((chunk + 2 * width, chans), F32),
            ((chunk, chans), F32),
            ((chunk, chans), BF16),
            ((chunk, chans), F32),
            ((chunk, ff), BF16),
            ((chans, ff), F32),
            ((ff, chans), F32),
        ],
        32,
    )
    mid = share_planes(share_cores(kept0, sent0))
    g1, win0, mix_bg0, conv_g1, small1 = call(
        window_back_kernel,
        units,
        near(g3, unit)
        + [
            rows_in(mask, unit),
            vec(1),
            vec(0),
            rows_in(x2, unit),
            rows_in(x1, unit),
            rows_in(nw, wrows),
            rows_in(mw, wrows),
            rows_in(ow, wrows),
            layer(mix_w, 0),
            layer(out_w, 0),
            whole(gather),
        ],
        [
            rows_out(chans, F32, unit),
            sums(4 * chans, chans, dtype=BF16),
            sums(8, 3 * chans),
            sums(72, chans),
            sums(32, chans),
        ],
        [
            ((unit + 2 * width, chans), F32),
            ((3 * chans, chans), F32),
            ((chans, chans), F32),
            ((unit, chans), F32),
            ((wrows, chans), BF16),
            ((wrows, chans), BF16),
            ((wrows, 3 * chans), BF16),
            ((unit, chans), F32),
            ((wrows * chans // LANES, 4 * SLOT), BF16),
            ((wrows * chans // LANES, 4 * SLOT), BF16),
        ],
        34,
    )
    mid, g1 = lax.optimization_barrier((mid, g1))
    x0_flat = x0.reshape(tokens, chans)
    sums1 = (conv_g1, conv_g2, conv_g3, small1, small3, small5, small6, small7, mix_bg0, mix_bg1, up_bg0, up_bg1)
    half = (win0.shape[0] + SMALL_ROWS) // 2
    tokens_grad, kept, sent = call(
        token_grad_kernel,
        chunks,
        near(g1, chunk)
        + [rows_in(mask, chunk), vec(0), rows_in(x0_flat, chunk), scalar, whole(win0)]
        + [whole(array) for array in sums1],
        [rows_out(chans, BF16), sums(half, chans, dtype=BF16), sums(half, chans, dtype=BF16)],
        [
            ((chunk + 2 * width, chans), F32),
            ((72, chans), F32),
            ((8, chans), F32),
            ((SMALL_ROWS, chans), F32),
        ],
        10,
        after=(result, *mid),
    )
    return result, tokens_grad, mid, kept, sent


def small_sums(
    core, win0, conv0, conv1, conv2, conv3, s0, s1, s3, s5, s6, s7, mix0, mix1, up0, up1,
    kept, sent, rows,
):
    chans = rows.shape[1]
    rows[...] = jnp.zeros_like(rows)
    place = 0

    def put(part):
        nonlocal place
        rows[place : place + 1, :] = jnp.sum(part, axis=0, keepdims=True)
        place += 1

    for conv in (conv0, conv1, conv2, conv3):
        for k in range(9):
            put(conv[8 * k : 8 * k + 8, :])
    for ref, at in (
        (s0, 0), (s1, 0), (s3, 0), (s6, 0),
        (s1, 16), (s3, 16), (s5, 0), (s7, 8),
        (s1, 24), (s3, 24), (s5, 8), (s7, 16),
        (s1, 8), (s6, 8), (s3, 8), (s7, 0),
    ):
        put(ref[at : at + 8, :])
    for ref in (mix0, mix1, up0, up1):
        for col in range(0, ref.shape[1], chans):
            put(ref[:, col : col + chans])
    spread(core, kept, sent, [win0, rows])


def reader(halves, plane, share, offset, stride, members):
    first = halves[0][0][0]
    part = members // 2 * stride
    planes = 2 * first.shape[0] // part
    bits = planes.bit_length() - 1

    def piece(at, take):
        n, inside = divmod(at, share)
        core, n = divmod(n, planes * members)
        owner, member = divmod(n, members)
        late, place = divmod(member * stride + offset + inside, part)
        far = plane ^ owner
        if late:
            far = sum(((far >> k) & 1) << (bits - 1 - k) for k in range(bits))
        near, other = halves[core][late]
        start = (far & (planes // 2 - 1)) * part + place
        rows = pl.ds(pl.multiple_of(start, 16), take)
        return jnp.where(far < planes // 2, near[rows, :], other[rows, :]).astype(F32)

    def read(at, rows):
        parts = []
        while rows:
            take = min(rows, share - at % share)
            parts.append(piece(at, take))
            at, rows = at + take, rows - take
        return parts[0] if len(parts) == 1 else jnp.concatenate(parts, axis=0)

    return read


def plain_reader(first, second):
    half = first.shape[0]

    def read(at, rows):
        parts = []
        if at < half:
            parts.append(first[at : min(at + rows, half), :].astype(F32))
        if at + rows > half:
            parts.append(second[max(at - half, 0) : at + rows - half, :].astype(F32))
        return parts[0] if len(parts) == 1 else jnp.concatenate(parts, axis=0)

    return read


def put_attention(read, mix_w, out_w):
    chans = out_w.shape[1]
    for k in range(3):
        mix_w[0, :, k * chans : (k + 1) * chans] = read(k * chans, chans)
    out_w[0] = read(3 * chans, chans)


def put_feed(read, at, up_w, down_w):
    chans = down_w.shape[2]
    blocks = up_w.shape[2] // chans
    for k in range(blocks):
        up_w[0, :, k * chans : (k + 1) * chans] = read(at + k * chans, chans)
    for k in range(blocks):
        down_w[0, k * chans : (k + 1) * chans, :] = read(at + (blocks + k) * chans, chans)


def final_kernel(
    place, *refs, shares, members,
):
    inputs, outs, rows = refs[:-15], refs[-15:-1], refs[-1]
    (
        mix_w, out_w, up_w, down_w, conv_w, conv_b, gain, shift, last_shift, win_b, chan_b, out_b, up_b, down_b,
    ) = outs
    layer = pl.program_id(0)
    chans = inputs[0].shape[1]
    feed_rows = 2 * up_w.shape[2]
    blocks = up_b.shape[1] // chans
    mid_share, late_share = shares
    stride = mid_share + late_share
    count = len(inputs) // 2
    here, there = inputs[:count], inputs[count:]

    for flag in range(2):
        halves = (here, there) if flag == 0 else (there, here)
        if count == 2:
            mid, late = (plain_reader(*pair) for pair in zip(*halves))
        else:
            pairs = tuple((half[0:2], half[2:4]) for half in halves)
            mid = reader(pairs, place[1], mid_share, 0, stride, members)
            late = reader(pairs, place[1], late_share, mid_share, stride, members)

        @pl.when((place[0] == flag) & (layer == 0))
        def _():
            put_attention(late, mix_w, out_w)
            put_feed(lambda at, count: mid(feed_rows + 4 * chans + at, count), 0, up_w, down_w)
            rows[...] = late(4 * chans, SMALL_ROWS)

        @pl.when((place[0] == flag) & (layer == 1))
        def _():
            put_attention(lambda at, count: mid(feed_rows + at, count), mix_w, out_w)
            put_feed(mid, 0, up_w, down_w)

    @pl.when(layer == 0)
    def _():
            at = 0
            for k in range(4):
                for i in range(3):
                    for j in range(3):
                        conv_w[i, j, k : k + 1, :] = rows[at : at + 1, :]
                        at += 1
            for ref in (conv_b, gain):
                ref[...] = rows[at : at + 4, :]
                at += 4
            shift[...] = rows[at : at + 3, :]
            last_shift[...] = rows[at + 3, :]
            at += 4
            for ref in (out_b, down_b):
                ref[...] = rows[at : at + 2, :]
                at += 2
            win_b[:chans] = rows[at, :]
            win_b[chans:] = rows[at + 2, :]
            for k in range(3):
                chan_b[k * chans : (k + 1) * chans] = rows[at + 3 + k, :]
            at += 6
            for k in range(2):
                for i in range(blocks):
                    up_b[k : k + 1, i * chans : (i + 1) * chans] = rows[at : at + 1, :]
                    at += 1


def assemble(place, arrays, shares, members, ff):
    chans = arrays[0].shape[1]
    shapes = [
        (2, chans, 3 * chans), (2, chans, chans), (2, chans, ff), (2, ff, chans),
        (3, 3, 4, chans), (4, chans), (4, chans), (3, chans), (chans,),
        (2 * chans,), (3 * chans,), (2, chans), (2, ff), (2, chans),
    ]

    def out_spec(shape):
        if len(shape) == 3:
            return pl.BlockSpec((1,) + shape[1:], lambda i: (i, 0, 0))
        return pl.BlockSpec(shape, lambda i: (0,) * len(shape))

    (
        mix_w, out_w, up_w, down_w, conv_w, conv_b, gain, shift, last_shift, win_b, chan_b, out_b, up_b, down_b,
    ) = pl.pallas_call(
        functools.partial(final_kernel, shares=shares, members=members),
        grid=(2,),
        in_specs=[pl.BlockSpec(memory_space=pltpu.SMEM)]
        + [pl.BlockSpec(x.shape, lambda i: (0, 0), pipeline_mode=pl.Buffered(1)) for x in arrays],
        out_specs=[out_spec(shape) for shape in shapes],
        out_shape=[jax.ShapeDtypeStruct(shape, F32) for shape in shapes],
        scratch_shapes=[pltpu.VMEM((SMALL_ROWS, chans), F32)],
        compiler_params=pltpu.CompilerParams(vmem_limit_bytes=VMEM_LIMIT),
    )(place, *arrays)
    return (
        conv_w.transpose(2, 0, 1, 3), conv_b, gain, shift, last_shift, mix_w,
        win_b, chan_b, out_w, out_b, up_w, up_b, down_w, down_b,
    )


def split_kernel(me, *refs, terms):
    outs = refs[terms:]
    rows = outs[0].shape[0]
    for step, out in enumerate(outs):
        at = pl.multiple_of((me[0] ^ step) * rows, 16)
        total = refs[0][pl.ds(at, rows), :].astype(F32)
        for ref in refs[1:terms]:
            total = total + ref[pl.ds(at, rows), :].astype(F32)
        out[...] = total.astype(BF16)


def split_sum(terms, me, size):
    rows, chans = terms[0].shape
    rows //= size
    if rows % 16 or rows < 512:
        total = functools.reduce(lambda x, y: x + y, [term.astype(F32) for term in terms]).astype(BF16)
        return [lax.dynamic_slice_in_dim(total, (me ^ step) * rows, rows, 0) for step in range(size)]
    return pl.pallas_call(
        functools.partial(split_kernel, terms=len(terms)),
        in_specs=[pl.BlockSpec(memory_space=pltpu.SMEM)] + [pl.BlockSpec(memory_space=pltpu.VMEM)] * len(terms),
        out_shape=[jax.ShapeDtypeStruct((rows, chans), BF16)] * size,
        compiler_params=pltpu.CompilerParams(vmem_limit_bytes=VMEM_LIMIT),
    )(me.astype(jnp.int32).reshape(1), *terms)


def widen_kernel(here, *refs):
    out = refs[-1]
    cols = out.shape[2]
    for step, part in enumerate(refs[:-1]):

        @pl.when(pl.program_id(0) == step)
        def _():
            out[0] = part[:, :cols, :]


def widen(parts, here, cols):
    images = len(parts)
    height, width, chans = parts[0].shape
    return pl.pallas_call(
        widen_kernel,
        grid_spec=pltpu.PrefetchScalarGridSpec(
            num_scalar_prefetch=1,
            grid=(images,),
            in_specs=[pl.BlockSpec(x.shape, lambda i, at: (0, 0, 0), pipeline_mode=pl.Buffered(1)) for x in parts],
            out_specs=pl.BlockSpec(
                (1, height, cols, chans), lambda i, at: ((at[0] + images - i) % images, 0, 0, 0)
            ),
        ),
        out_shape=jax.ShapeDtypeStruct((images, height, cols, chans), BF16),
        compiler_params=pltpu.CompilerParams(vmem_limit_bytes=VMEM_LIMIT),
    )(here.astype(jnp.int32).reshape(1), *parts)


def local(
    tokens, heights, conv_weight, conv_bias, norm_gain, norm_shift, mix_weight, window_bias, channel_bias,
    out_weight, out_bias, up_weight, up_bias, down_weight, down_bias, cotangent,
):
    images, height, cols, chans = tokens.shape
    count = lax.axis_size("rows")
    place = lax.axis_index("rows")
    width = -(-cols // 8) * 8
    groups = count // images
    members = [[g * images + j for j in range(images)] for g in range(groups)]
    rows_here = images * height
    level = lax.dynamic_index_in_dim(heights, place % images, 0, keepdims=False)
    open_rows = heights * 7 - place * height

    def pad_image(field):
        inside = jnp.arange(height, dtype=jnp.int32)[None, :] < open_rows[:, None]
        field = jnp.where(inside[:, :, None, None], field, jnp.zeros((), field.dtype))
        return jnp.pad(field, ((0, 0), (0, 0), (0, width - cols), (0, 0)))

    def spread_image(field):
        field = lax.all_to_all(field, "rows", 0, 0, axis_index_groups=members, tiled=True)
        return field.reshape(rows_here, width, chans)

    def scatter_image(field):
        field = field.reshape(images, height, width, chans)
        field = lax.all_to_all(field, "rows", 0, 0, axis_index_groups=members, tiled=True)
        return field[:, :, :cols]

    def halo_of(field):
        flat = field.reshape(rows_here * width, chans)
        if groups == 1:
            return jnp.zeros((2 * width, chans), F32)
        down = [(i, i + images) for i in range(count - images)]
        up = [(i + images, i) for i in range(count - images)]
        above = lax.ppermute(flat[-width:].astype(BF16), "rows", down)
        below = lax.ppermute(flat[:width].astype(BF16), "rows", up)
        return jnp.concatenate([above, below], axis=0).astype(F32)

    def across(value):
        if groups == 1:
            return value
        other = [[j + g * images for g in range(groups)] for j in range(images)]
        return lax.psum(value, "rows", axis_index_groups=other)

    row = jnp.arange(rows_here * width, dtype=jnp.int32) // width + place // images * rows_here
    col = jnp.arange(rows_here * width, dtype=jnp.int32) % width
    mask = ((row < level * 7) & (col < cols)).astype(F32)
    mask = jnp.broadcast_to(mask[:, None], (rows_here * width, LANES))
    scale = lax.rsqrt((level * 7 * cols).astype(F32))
    scale = jnp.broadcast_to(scale, (8, LANES))
    small = prepare(conv_weight, conv_bias, norm_gain, norm_shift, out_bias, down_bias, up_bias)
    small += (
        jnp.concatenate([window_bias[:chans], jnp.zeros((chans,), BF16), window_bias[chans:]]).astype(F32)[None],
        channel_bias.astype(F32)[None],
    )
    x0 = spread_image(pad_image(tokens))
    cot, small, mask, scale = lax.optimization_barrier((pad_image(cotangent), small, mask, scale))
    cot = spread_image(cot).reshape(rows_here * width, chans)

    def exchange(part, axis, step):
        size = lax.axis_size(axis)
        return lax.ppermute(part, axis, [(i, i ^ step) for i in range(size)])

    core = lax.axis_index("core").astype(jnp.int32).reshape(1)

    def share(terms, axis):
        size = lax.axis_size(axis)
        pieces = split_sum(terms, lax.axis_index(axis), size)
        return [pieces[0]] + [exchange(pieces[step], axis, step) for step in range(1, size)]

    def share_cores(kept, sent):
        return [kept, exchange(sent, "core", 1)]

    def total(terms):
        return functools.reduce(lambda x, y: x + y, [term.astype(F32) for term in terms]).astype(BF16)

    def gather(part, axis):
        size, me = lax.axis_size(axis), lax.axis_index(axis)
        rows = part.shape[0]
        out = jnp.zeros((size * rows, part.shape[1]), part.dtype)
        for step in range(size):
            got = part if step == 0 else exchange(part, axis, step)
            out = lax.dynamic_update_slice_in_dim(out, got, (me ^ step) * rows, 0)
        return out

    def join(part, other):
        rows = part.shape[0]
        out = jnp.zeros((2 * rows, part.shape[1]), part.dtype)
        out = lax.dynamic_update_slice_in_dim(out, part, 0, 0)
        return lax.dynamic_update_slice_in_dim(out, other, rows, 0)

    def send_tokens(field):
        field = field.reshape(images, height, width, chans)
        here = place % images
        parts = []
        for step in range(images):
            part = lax.dynamic_index_in_dim(field, (here + step) % images, 0, keepdims=False)
            if step:
                pairs = [(g * images + j, g * images + (j + step) % images) for g in range(groups) for j in range(images)]
                part = lax.ppermute(part, "rows", pairs)
            parts.append(part)
        return parts

    weights = (mix_weight, out_weight, up_weight, down_weight)
    result, tokens_grad, mid, kept, sent = image_block(
        x0, cot, halo_of(x0), mask, scale, halo_of, across, weights, small, cols, core,
        scatter_image, share_cores, lambda terms: share(terms, "plane"),
    )
    together = lax.optimization_barrier
    tokens_grad = send_tokens(tokens_grad)
    mid = share(mid, "rows")
    kept, sent, mid = together((kept, sent, mid))
    late = share(share_cores(kept, sent), "plane")
    late, tokens_grad[2:3] = together((late, tokens_grad[2:3]))
    late = total(share(late, "rows"))
    mid = total(mid)
    shares = (mid.shape[0], late.shape[0])
    block = gather(jnp.concatenate([mid, late], axis=0), "rows")
    members = lax.axis_size("rows")
    bits = lax.axis_size("plane").bit_length() - 1
    half = block.shape[0] // 2
    parts = [block[:half], block[half:]]
    aligned = all(rows % 16 == 0 for rows in shares)
    if not aligned:
        block = gather(block, "plane").reshape(-1, sum(shares), chans)
        arrays = [block[:, : shares[0]].reshape(-1, chans), block[:, shares[0] :].reshape(-1, chans)]
        tokens_grad = widen(tokens_grad, place % images, cols)
    for k in range(bits if aligned else 0):
        others = [exchange(part, "plane", 1 << bit) for part, bit in zip(parts, (k, bits - 1 - k))]
        if k == bits - 1:
            tokens_grad = widen(tokens_grad, place % images, cols)
            others, tokens_grad = together((others, tokens_grad))
        if k + 1 < bits:
            parts = [join(part, other) for part, other in zip(parts, others)]
        else:
            arrays = [parts[0], others[0], parts[1], others[1]]
    arrays += [exchange(array, "core", 1) for array in arrays]
    at = jnp.concatenate([core, lax.axis_index("plane").astype(jnp.int32).reshape(1)])
    return result, tokens_grad.astype(F32), *assemble(at, arrays, shares, members, up_weight.shape[2])


def solution(mesh):
    planes = mesh.shape["dp"] // 2
    fine = Mesh(mesh.devices.reshape(planes, 2, mesh.shape["rows"]), ("plane", "core", "rows"))
    dp = ("plane", "core")
    split = P(dp, "rows", None, None)
    in_specs = (split, P(dp)) + (P(),) * 13 + (split,)
    out_specs = (split, split) + (P(),) * 14
    return jax.shard_map(local, mesh=fine, in_specs=in_specs, out_specs=out_specs, check_vma=False)
```

profile of v0, /device:TPU:0, one launch (start us, length us, event | category | flops | bytes accessed | tf_op | source)
XLA Modules:
  0.0 387.4 jit_solution(8175759265833554980)
XLA Ops:
  1.4 2.5 copy_select_fusion
  5.1 6.4 %all-to-all-start = ((bf16[4,7,72,384]{3,2,1,0:T(8,128)(2,1)}), bf16[4,7,72,384]{3,2,1,0:T(8,128)(2,1)S(1)}, u32[]{:S(2)}, u32[]{:S(2)}) async-start(bf16[4,7,72,384]{3,2,1,0:T(8,128)(2,1)} %pad.9), calls=%async_computation | async-start | bytes 3096576 | tf_op jit(solution)/shard_map/all_to_all | solution.py:1193
  13.5 1.3 pad.10
  16.1 1.5 shard_map.288
  20.1 27.9 %all-to-all-done = bf16[4,7,72,384]{3,2,1,0:T(8,128)(2,1)S(1)} async-done(((bf16[4,7,72,384]{3,2,1,0:T(8,128)(2,1)}), bf16[4,7,72,384]{3,2,1,0:T(8,128)(2,1)S(1)}, u32[]{:S(2)}, u32[]{:S(2)}) %all-to-all-start) | async-done | bytes 1548320 | tf_op jit(solution)/shard_map/all_to_all | solution.py:1193
  48.0 3.6 all-to-all-start.1
  52.3 19.6 %shard_map.289 = (f32[2016,384]{1,0:T(8,128)}, bf16[2560,384]{1,0:T(8,128)(2,1)}, bf16[2560,1152]{1,0:T(8,128)(2,1)}, bf16[2560,384]{1,0:T(8,128)(2,1)}, f32[2016,384]{1,0:T(8,128)}) custom-call(bf16[28,72,384]{2,1,0:T(8,128)(2,1)} %bitcast.20, bf16[28,72,384]{2,1,0:T(8,128)(2,1)} %bitcast.21, bf16[28,72,384]{2,1,0:T(8,128)(2,1)} %bitcast.22, ...), custom_call_target="tpu_custom_call" | custom-call | flops 1 | bytes 72000000 | tf_op jit(solution)/shard_map/pallas_call | solution.py:597
  71.9 24.7 %shard_map.290 = (f32[2016,384]{1,0:T(8,128)}, f32[2016,384]{1,0:T(8,128)}, bf16[2016,384]{1,0:T(8,128)(2,1)}, bf16[2016,1536]{1,0:T(8,128)(2,1)}, bf16[2016,1536]{1,0:T(8,128)(2,1)}) custom-call(f32[2016,384]{1,0:T(8,128)} %get-tuple-element.112.refs_0_.refs_1_.refs_2_.refs_7_, f32[2016,384]{1,0:T(8,128)} %get-tuple-element.112.refs_0_.refs_1_.refs_2_.refs_7_, ...), custom_call_target="tpu_custom_call" | custom-call | flops 1 | bytes 90000000 | tf_op jit(solution)/shard_map/pallas_call | solution.py:597
  96.6 11.3 %shard_map.291 = (f32[2016,384]{1,0:T(8,128)}, bf16[2016,384]{1,0:T(8,128)(2,1)}, bf16[2016,1152]{1,0:T(8,128)(2,1)}, f32[3,128,128]{2,1,0:T(8,128)}) custom-call(f32[2016,384]{1,0:T(8,128)} %get-tuple-element.114.refs_0_.refs_1_.refs_2_.refs_7_, f32[2016,384]{1,0:T(8,128)} %get-tuple-element.114.refs_0_.refs_1_.refs_2_.refs_7_, ...), custom_call_target="tpu_custom_call" | custom-call | flops 1 | bytes 39600000 | tf_op jit(solution)/shard_map/pallas_call | solution.py:597
  108.0 6.6 %shard_map.292 = (bf16[2016,384]{1,0:T(8,128)(2,1)}, f32[2016,384]{1,0:T(8,128)}) custom-call(bf16[2016,1152]{1,0:T(8,128)(2,1)} %get-tuple-element.116.refs_0_.refs_7_.refs_1_, f32[3,128,128]{2,1,0:T(8,128)} %get-tuple-element.117.refs_1_.refs_2_, f32[8,128]{1,0:T(8,128)} %broadcast_in_dim.47.refs_2_.refs_4_, ...), custom_call_target="tpu_custom_call" | custom-call | flops 1 | bytes 25200000 | tf_op jit(solution)/shard_map/pallas_call | solution.py:597
  115.7 39.3 %shard_map.293 = (bf16[2016,384]{1,0:T(8,128)(2,1)}, f32[2016,384]{1,0:T(8,128)}, bf16[3072,384]{1,0:T(8,128)(2,1)}, f32[8,1536]{1,0:T(8,128)}, f32[24,384]{1,0:T(8,128)}) custom-call(f32[2016,384]{1,0:T(8,128)} %get-tuple-element.120.refs_0_.refs_1_.refs_2_.refs_6_, f32[2016,384]{1,0:T(8,128)} %get-tuple-element.120.refs_0_.refs_1_.refs_2_.refs_6_, ...), custom_call_target="tpu_custom_call" | custom-call | flops 1 | bytes 136800000 | tf_op jit(solution)/shard_map/pallas_call | solution.py:597
  155.0 13.3 %shard_map.294 = (f32[2016,384]{1,0:T(8,128)}, bf16[2016,384]{1,0:T(8,128)(2,1)}, f32[3,128,128]{2,1,0:T(8,128)}, bf16[384,384]{1,0:T(8,128)(2,1)}, f32[72,384]{1,0:T(8,128)}, /*index=5*/f32[16,384]{1,0:T(8,128)}) custom-call(f32[2016,384]{1,0:T(8,128)} %get-tuple-element.123.refs_0_.refs_1_.refs_2_, f32[2016,384]{1,0:T(8,128)} %get-tuple-element.123.refs_0_.refs_1_.refs_2_, ...), custom_call_target="tpu_custom_call" | custom-call | flops 1 | bytes 46800000 | tf_op jit(solution)/shard_map/pallas_call | solution.py:597
  168.3 15.6 %shard_map.295 = (f32[2016,384]{1,0:T(8,128)}, bf16[1152,384]{1,0:T(8,128)(2,1)}, f32[8,1152]{1,0:T(8,128)}, f32[16,384]{1,0:T(8,128)}) custom-call(bf16[2016,384]{1,0:T(8,128)(2,1)} %get-tuple-element.125.refs_0_, bf16[2016,1152]{1,0:T(8,128)(2,1)} %get-tuple-element.116.refs_0_.refs_7_.refs_1_, f32[3,128,128]{2,1,0:T(8,128)} %get-tuple-element.117.refs_1_.refs_2_, ...), custom_call_target="tpu_custom_call" | custom-call | flops 1 | bytes 57600000 | tf_op jit(solution)/shard_map/pallas_call | solution.py:597
  183.9 31.9 %shard_map.296 = (f32[2016,384]{1,0:T(8,128)}, bf16[3840,384]{1,0:T(8,128)(2,1)}, bf16[3840,384]{1,0:T(8,128)(2,1)}, f32[8,1536]{1,0:T(8,128)}, f32[72,384]{1,0:T(8,128)}, /*index=5*/f32[32,384]{1,0:T(8,128)}) custom-call(f32[2016,384]{1,0:T(8,128)} %get-tuple-element.129.refs_0_.refs_1_.refs_2_, f32[2016,384]{1,0:T(8,128)} %get-tuple-element.129.refs_0_.refs_1_.refs_2_, ...), custom_call_target="tpu_custom_call" | custom-call | flops 1 | bytes 115200000 | tf_op jit(solution)/shard_map/pallas_call | solution.py:597
  215.8 5.2 %all-to-all-start.2 = ((bf16[4,7,72,384]{3,2,1,0:T(8,128)(2,1)}), bf16[4,7,72,384]{3,2,1,0:T(8,128)(2,1)S(1)}, u32[]{:S(2)}, u32[]{:S(2)}) async-start(bf16[4,7,72,384]{3,2,1,0:T(8,128)(2,1)} %bitcast.4), calls=%async_computation.2 | async-start | bytes 3096576 | tf_op jit(solution)/shard_map/all_to_all | solution.py:1198
  221.5 4.6 %shard_map.297 = (bf16[960,384]{1,0:T(8,128)(2,1)}, bf16[960,384]{1,0:T(8,128)(2,1)}, bf16[960,384]{1,0:T(8,128)(2,1)}, bf16[960,384]{1,0:T(8,128)(2,1)}) custom-call(s32[1]{0:T(128)} %bitcast.5.me, bf16[3840,384]{1,0:T(8,128)(2,1)} %get-tuple-element.137.refs_0_, bf16[3840,384]{1,0:T(8,128)(2,1)} %collective-permute-done.refs_1_), custom_call_target="tpu_custom_call" | custom-call | tf_op jit(solution)/shard_map/pallas_call | solution.py:1137
  226.1 1.5 collective-permute-start.1
  227.6 1.5 collective-permute-start.2
  229.6 33.9 %shard_map.298 = (f32[2016,384]{1,0:T(8,128)}, bf16[1536,384]{1,0:T(8,128)(2,1)}, f32[8,1152]{1,0:T(8,128)}, f32[72,384]{1,0:T(8,128)}, f32[32,384]{1,0:T(8,128)}) custom-call(f32[2016,384]{1,0:T(8,128)} %get-tuple-element.143.refs_0_.refs_1_.refs_2_, f32[2016,384]{1,0:T(8,128)} %get-tuple-element.143.refs_0_.refs_1_.refs_2_, ...), custom_call_target="tpu_custom_call" | custom-call | flops 1 | bytes 122400000 | tf_op jit(solution)/shard_map/pallas_call | solution.py:597
  263.6 2.0 add_convert_fusion.1
  266.4 2.0 collective-permute-start.4
  268.3 2.4 collective-permute-start.5
  271.9 9.9 %shard_map.299 = (bf16[2016,384]{1,0:T(8,128)(2,1)}, bf16[1024,384]{1,0:T(8,128)(2,1)}, bf16[1024,384]{1,0:T(8,128)(2,1)}) custom-call(f32[2016,384]{1,0:T(8,128)} %get-tuple-element.149.refs_0_.refs_1_.refs_2_, f32[2016,384]{1,0:T(8,128)} %get-tuple-element.149.refs_0_.refs_1_.refs_2_, f32[2016,384]{1,0:T(8,128)} %get-tuple-element.149.refs_0_.refs_1_.refs_2_, ...), custom_call_target="tpu_custom_call" | custom-call | flops 1 | bytes 36000000 | tf_op jit(solution)/shard_map/pallas_call | solution.py:597
  281.8 2.9 collective-permute-done.5
  284.8 2.3 dynamic-slice_bitcast_fusion
  287.1 3.4 collective-permute-start.11
  290.9 2.5 collective-permute-start.10
  294.5 14.1 %collective-permute-done.11.refs_2_ = bf16[7,72,384]{2,1,0:T(8,128)(2,1)S(1)} collective-permute-done((bf16[7,72,384]{2,1,0:T(8,128)(2,1)S(1)}, bf16[7,72,384]{2,1,0:T(8,128)(2,1)S(1)}, u32[]{:S(2)}, u32[]{:S(2)}) %collective-permute-start.11) | collective-permute-done | bytes 387104 | tf_op jit(solution)/shard_map/ppermute | solution.py:1272
  308.8 2.0 collective-permute-start.13
  310.8 2.4 collective-permute-start.14
  314.4 2.3 collective-permute-done.14
  317.0 2.9 collective-permute-start.16
  319.9 1.5 collective-permute-start.17
  321.3 5.6 %collective-permute-done.15 = bf16[304,384]{1,0:T(8,128)(2,1)S(1)} collective-permute-done((bf16[304,384]{1,0:T(8,128)(2,1)S(1)}, bf16[304,384]{1,0:T(8,128)(2,1)S(1)}, u32[]{:S(2)}, u32[]{:S(2)}) %collective-permute-start.15) | collective-permute-done | bytes 233504 | tf_op jit(solution)/shard_map/ppermute | solution.py:1234
  327.0 9.5 %collective-permute-done.16 = bf16[304,384]{1,0:T(8,128)(2,1)S(1)} collective-permute-done((bf16[304,384]{1,0:T(8,128)(2,1)S(1)}, bf16[304,384]{1,0:T(8,128)(2,1)S(1)}, u32[]{:S(2)}, u32[]{:S(2)}) %collective-permute-start.16) | collective-permute-done | bytes 233504 | tf_op jit(solution)/shard_map/ppermute | solution.py:1234
  336.8 1.6 collective-permute-start.20
  338.4 1.5 collective-permute-start.18
  339.9 6.6 %collective-permute-done.20 = bf16[608,384]{1,0:T(8,128)(2,1)S(1)} collective-permute-done((bf16[608,384]{1,0:T(8,128)(2,1)S(1)}, bf16[608,384]{1,0:T(8,128)(2,1)S(1)}, u32[]{:S(2)}, u32[]{:S(2)}) %collective-permute-start.20) | collective-permute-done | bytes 466976 | tf_op jit(solution)/shard_map/ppermute | solution.py:1234
  346.6 1.7 collective-permute-start.21
  348.3 3.1 collective-permute-done.18
  351.6 2.2 collective-permute-start.22
  353.8 1.7 collective-permute-start.23
  355.5 7.1 %collective-permute-done.22.refs_1_ = bf16[7,72,384]{2,1,0:T(8,128)(2,1)S(1)} collective-permute-done((bf16[7,72,384]{2,1,0:T(8,128)(2,1)S(1)}, bf16[7,72,384]{2,1,0:T(8,128)(2,1)S(1)}, u32[]{:S(2)}, u32[]{:S(2)}) %collective-permute-start.22) | collective-permute-done | bytes 387104 | tf_op jit(solution)/shard_map/ppermute | solution.py:1272
  362.7 4.2 %collective-permute-done.23.refs_3_ = bf16[7,72,384]{2,1,0:T(8,128)(2,1)S(1)} collective-permute-done((bf16[7,72,384]{2,1,0:T(8,128)(2,1)S(1)}, bf16[7,72,384]{2,1,0:T(8,128)(2,1)S(1)}, u32[]{:S(2)}, u32[]{:S(2)}) %collective-permute-start.23) | collective-permute-done | bytes 387104 | tf_op jit(solution)/shard_map/ppermute | solution.py:1272
  367.6 3.1 shard_map.300
  372.4 1.7 copy.42
  374.1 2.2 copy.43
  378.3 8.9 %shard_map.301 = (f32[2,384,1152]{2,1,0:T(8,128)}, f32[2,384,384]{2,1,0:T(8,128)}, f32[2,384,1536]{2,1,0:T(8,128)}, f32[2,1536,384]{2,1,0:T(8,128)}, f32[3,3,4,3...) custom-call(s32[2]{0:T(128)} %pad_add_fusion.place, ...), custom_call_target="tpu_custom_call" | custom-call | tf_op jit(solution)/shard_map/pallas_call | solution.py:1104
  (116 shorter events, 19.2 us)
Async XLA Ops:
  5.1 6.5 %copy-start.24 = (s32[4]{0:T(128)S(1)}, s32[4]{0:T(128)}, u32[]{:S(2)}) copy-start(s32[4]{0:T(128)} %param.18) | copy-start | bytes 52
  5.1 42.9 %all-to-all-start = ((bf16[4,7,72,384]{3,2,1,0:T(8,128)(2,1)}), bf16[4,7,72,384]{3,2,1,0:T(8,128)(2,1)S(1)}, u32[]{:S(2)}, u32[]{:S(2)}) async-start(bf16[4,7,72,384]{3,2,1,0:T(8,128)(2,1)} %pad.9), calls=%async_computation | async-start | bytes 3096576 | tf_op jit(solution)/shard_map/all_to_all | solution.py:1193
  11.6 3.3 copy-start.23
  11.6 3.3 copy-start.21
  48.0 4.3 %copy-start = (bf16[4,7,72,384]{3,2,1,0:T(8,128)(2,1)}, bf16[4,7,72,384]{3,2,1,0:T(8,128)(2,1)S(1)}, u32[]{:S(2)}) copy-start(bf16[4,7,72,384]{3,2,1,0:T(8,128)(2,1)S(1)} %all-to-all-done) | copy-start | bytes 4644868
  48.0 66.5 %all-to-all-start.1 = ((bf16[4,7,72,384]{3,2,1,0:T(8,128)(2,1)}), bf16[4,7,72,384]{3,2,1,0:T(8,128)(2,1)S(1)}, u32[]{:S(2)}, u32[]{:S(2)}) async-start(bf16[4,7,72,384]{3,2,1,0:T(8,128)(2,1)} %pad.10), calls=%async_computation.1 | async-start | bytes 3096576 | tf_op jit(solution)/shard_map/all_to_all | solution.py:1193
  215.8 5.8 %collective-permute-start = (bf16[3840,384]{1,0:T(8,128)(2,1)}, bf16[3840,384]{1,0:T(8,128)(2,1)}, u32[]{:S(2)}, u32[]{:S(2)}) collective-permute-start(bf16[3840,384]{1,0:T(8,128)(2,1)} %get-tuple-element.138), channel_id=1, source_target_pairs={{0,4},{4,0},{1,5},{5,1},{2,6},{6,2},{3,7},{7,3},{8,12},{12,8},{9,1... | collective-permute-start | bytes 8847368 | tf_op jit(solution)/shard_map/ppermute | solution.py:1234
  215.8 54.9 %all-to-all-start.2 = ((bf16[4,7,72,384]{3,2,1,0:T(8,128)(2,1)}), bf16[4,7,72,384]{3,2,1,0:T(8,128)(2,1)S(1)}, u32[]{:S(2)}, u32[]{:S(2)}) async-start(bf16[4,7,72,384]{3,2,1,0:T(8,128)(2,1)} %bitcast.4), calls=%async_computation.2 | async-start | bytes 3096576 | tf_op jit(solution)/shard_map/all_to_all | solution.py:1198
  226.1 37.4 %collective-permute-start.1 = (bf16[960,384]{1,0:T(8,128)(2,1)}, bf16[960,384]{1,0:T(8,128)(2,1)S(1)}, u32[]{:S(2)}, u32[]{:S(2)}) collective-permute-start(bf16[960,384]{1,0:T(8,128)(2,1)} %get-tuple-element.140), channel_id=1, source_target_pairs={{0,8},{8,0},{16,24},{24,16},{1,9},{9,1},{17,25},{25,17},{2,10},{10... | collective-permute-start | bytes 2211848 | tf_op jit(solution)/shard_map/ppermute | solution.py:1234
  227.6 36.0 %collective-permute-start.2 = (bf16[960,384]{1,0:T(8,128)(2,1)}, bf16[960,384]{1,0:T(8,128)(2,1)}, u32[]{:S(2)}, u32[]{:S(2)}) collective-permute-start(bf16[960,384]{1,0:T(8,128)(2,1)} %get-tuple-element.141), channel_id=1, source_target_pairs={{0,16},{8,24},{16,0},{24,8},{1,17},{9,25},{17,1},{25,9},{2,18},{10... | collective-permute-start | bytes 2211848 | tf_op jit(solution)/shard_map/ppermute | solution.py:1234
  229.2 34.5 %collective-permute-start.3 = (bf16[960,384]{1,0:T(8,128)(2,1)}, bf16[960,384]{1,0:T(8,128)(2,1)}, u32[]{:S(2)}, u32[]{:S(2)}) collective-permute-start(bf16[960,384]{1,0:T(8,128)(2,1)} %get-tuple-element.142), channel_id=1, source_target_pairs={{0,24},{8,16},{16,8},{24,0},{1,25},{9,17},{17,9},{25,1},{2,26},{10... | collective-permute-start | bytes 2211848 | tf_op jit(solution)/shard_map/ppermute | solution.py:1234
  229.6 34.0 %copy-start.7 = (bf16[960,384]{1,0:T(8,128)(2,1)S(1)}, bf16[960,384]{1,0:T(8,128)(2,1)}, u32[]{:S(2)}) copy-start(bf16[960,384]{1,0:T(8,128)(2,1)} %get-tuple-element.163.refs_22_) | copy-start | bytes 2211844
  266.4 15.4 %collective-permute-start.4 = (bf16[240,384]{1,0:T(8,128)(2,1)}, bf16[240,384]{1,0:T(8,128)(2,1)S(1)}, u32[]{:S(2)}, u32[]{:S(2)}) collective-permute-start(bf16[240,384]{1,0:T(8,128)(2,1)} %get-tuple-element.242), channel_id=1, source_target_pairs={{0,1},{1,0},{2,3},{3,2},{4,5},{5,4},{6,7},{7,6},{8,9},{9,8},{10,11... | collective-permute-start | bytes 552968 | tf_op jit(solution)/shard_map/ppermute | solution.py:1234
  268.3 16.4 %collective-permute-start.5 = (bf16[240,384]{1,0:T(8,128)(2,1)S(1)}, bf16[240,384]{1,0:T(8,128)(2,1)S(1)}, u32[]{:S(2)}, u32[]{:S(2)}) collective-permute-start(bf16[240,384]{1,0:T(8,128)(2,1)S(1)} %get-tuple-element.241), channel_id=1, source_target_pairs={{0,2},{1,3},{2,0},{3,1},{4,6},{5,7},{6,4},{7,5},{8,10},{9,11},{10,... | collective-permute-start | bytes 552968 | tf_op jit(solution)/shard_map/ppermute | solution.py:1234
  270.7 14.0 %collective-permute-start.6 = (bf16[240,384]{1,0:T(8,128)(2,1)S(1)}, bf16[240,384]{1,0:T(8,128)(2,1)}, u32[]{:S(2)}, u32[]{:S(2)}) collective-permute-start(bf16[240,384]{1,0:T(8,128)(2,1)S(1)} %get-tuple-element.240), channel_id=1, source_target_pairs={{0,3},{1,2},{2,1},{3,0},{4,7},{5,6},{6,5},{7,4},{8,11},{9,10},{10,... | collective-permute-start | bytes 552968 | tf_op jit(solution)/shard_map/ppermute | solution.py:1234
  281.8 5.4 %copy-start.18 = (bf16[240,384]{1,0:T(8,128)(2,1)}, bf16[240,384]{1,0:T(8,128)(2,1)S(1)}, u32[]{:S(2)}) copy-start(bf16[240,384]{1,0:T(8,128)(2,1)S(1)} %collective-permute-done.4) | copy-start | bytes 552964
  284.7 2.4 copy-start.20
  284.7 5.9 %collective-permute-start.7 = (bf16[1024,384]{1,0:T(8,128)(2,1)}, bf16[1024,384]{1,0:T(8,128)(2,1)S(1)}, u32[]{:S(2)}, u32[]{:S(2)}) collective-permute-start(bf16[1024,384]{1,0:T(8,128)(2,1)} %get-tuple-element.174), channel_id=1, source_target_pairs={{0,4},{4,0},{1,5},{5,1},{2,6},{6,2},{3,7},{7,3},{8,12},{12,8},{9,1... | collective-permute-start | bytes 2359304 | tf_op jit(solution)/shard_map/ppermute | solution.py:1234
  284.8 5.8 %copy-start.14 = (bf16[1024,384]{1,0:T(8,128)(2,1)S(1)}, bf16[1024,384]{1,0:T(8,128)(2,1)}, u32[]{:S(2)}) copy-start(bf16[1024,384]{1,0:T(8,128)(2,1)} %get-tuple-element.173) | copy-start | bytes 2359300
  287.1 21.4 %collective-permute-start.11 = (bf16[7,72,384]{2,1,0:T(8,128)(2,1)S(1)}, bf16[7,72,384]{2,1,0:T(8,128)(2,1)S(1)}, u32[]{:S(2)}, u32[]{:S(2)}) collective-permute-start(bf16[7,72,384]{2,1,0:T(8,128)(2,1)S(1)} %get-tuple-element.233), channel_id=1, source_target_pairs={{0,2},{1,3},{2,0},{3,1},{4,6},{5,7},{6,4},{7,5},{8,10},{9,11},{10,... | collective-permute-start | bytes 1161224 | tf_op jit(solution)/shard_map/ppermute | solution.py:1272
  290.8 22.4 %copy-start.19 = (bf16[240,384]{1,0:T(8,128)(2,1)S(1)}, bf16[240,384]{1,0:T(8,128)(2,1)}, u32[]{:S(2)}) copy-start(bf16[240,384]{1,0:T(8,128)(2,1)} %copy-done.18) | copy-start | bytes 552964
  290.9 17.6 %collective-permute-start.10 = (bf16[256,384]{1,0:T(8,128)(2,1)S(1)}, bf16[256,384]{1,0:T(8,128)(2,1)S(1)}, u32[]{:S(2)}, u32[]{:S(2)}) collective-permute-start(bf16[256,384]{1,0:T(8,128)(2,1)S(1)} %get-tuple-element.236), channel_id=1, source_target_pairs={{0,24},{8,16},{16,8},{24,0},{1,25},{9,17},{17,9},{25,1},{2,26},{10... | collective-permute-start | bytes 589832 | tf_op jit(solution)/shard_map/ppermute | solution.py:1234
  293.4 15.1 %collective-permute-start.8 = (bf16[256,384]{1,0:T(8,128)(2,1)S(1)}, bf16[256,384]{1,0:T(8,128)(2,1)S(1)}, u32[]{:S(2)}, u32[]{:S(2)}) collective-permute-start(bf16[256,384]{1,0:T(8,128)(2,1)S(1)} %get-tuple-element.238), channel_id=1, source_target_pairs={{0,8},{8,0},{16,24},{24,16},{1,9},{9,1},{17,25},{25,17},{2,10},{10... | collective-permute-start | bytes 589832 | tf_op jit(solution)/shard_map/ppermute | solution.py:1234
  293.9 14.6 %collective-permute-start.9 = (bf16[256,384]{1,0:T(8,128)(2,1)S(1)}, bf16[256,384]{1,0:T(8,128)(2,1)S(1)}, u32[]{:S(2)}, u32[]{:S(2)}) collective-permute-start(bf16[256,384]{1,0:T(8,128)(2,1)S(1)} %get-tuple-element.237), channel_id=1, source_target_pairs={{0,16},{8,24},{16,0},{24,8},{1,17},{9,25},{17,1},{25,9},{2,18},{10... | collective-permute-start | bytes 589832 | tf_op jit(solution)/shard_map/ppermute | solution.py:1234
  308.5 8.3 %copy-start.15 = (bf16[7,72,384]{2,1,0:T(8,128)(2,1)}, bf16[7,72,384]{2,1,0:T(8,128)(2,1)S(1)}, u32[]{:S(2)}) copy-start(bf16[7,72,384]{2,1,0:T(8,128)(2,1)S(1)} %collective-permute-done.11.refs_2_) | copy-start | bytes 1161220
  308.7 5.6 %collective-permute-start.12 = (bf16[64,384]{1,0:T(8,128)(2,1)S(1)}, bf16[64,384]{1,0:T(8,128)(2,1)S(1)}, u32[]{:S(2)}, u32[]{:S(2)}) collective-permute-start(bf16[64,384]{1,0:T(8,128)(2,1)S(1)} %get-tuple-element.246), channel_id=1, source_target_pairs={{0,1},{1,0},{2,3},{3,2},{4,5},{5,4},{6,7},{7,6},{8,9},{9,8},{10,11... | collective-permute-start | bytes 147464 | tf_op jit(solution)/shard_map/ppermute | solution.py:1234
  308.8 5.6 %collective-permute-start.13 = (bf16[64,384]{1,0:T(8,128)(2,1)S(1)}, bf16[64,384]{1,0:T(8,128)(2,1)S(1)}, u32[]{:S(2)}, u32[]{:S(2)}) collective-permute-start(bf16[64,384]{1,0:T(8,128)(2,1)S(1)} %get-tuple-element.248), channel_id=1, source_target_pairs={{0,2},{1,3},{2,0},{3,1},{4,6},{5,7},{6,4},{7,5},{8,10},{9,11},{10,... | collective-permute-start | bytes 147464 | tf_op jit(solution)/shard_map/ppermute | solution.py:1234
  310.8 5.9 %collective-permute-start.14 = (bf16[64,384]{1,0:T(8,128)(2,1)S(1)}, bf16[64,384]{1,0:T(8,128)(2,1)S(1)}, u32[]{:S(2)}, u32[]{:S(2)}) collective-permute-start(bf16[64,384]{1,0:T(8,128)(2,1)S(1)} %get-tuple-element.247), channel_id=1, source_target_pairs={{0,3},{1,2},{2,1},{3,0},{4,7},{5,6},{6,5},{7,4},{8,11},{9,10},{10,... | collective-permute-start | bytes 147464 | tf_op jit(solution)/shard_map/ppermute | solution.py:1234
  316.9 10.1 %collective-permute-start.15 = (bf16[304,384]{1,0:T(8,128)(2,1)S(1)}, bf16[304,384]{1,0:T(8,128)(2,1)S(1)}, u32[]{:S(2)}, u32[]{:S(2)}) collective-permute-start(bf16[304,384]{1,0:T(8,128)(2,1)S(1)} %get-tuple-element.244), channel_id=1, source_target_pairs={{0,1},{1,0},{2,3},{3,2},{4,5},{5,4},{6,7},{7,6},{8,9},{9,8},{10,11... | collective-permute-start | bytes 700424 | tf_op jit(solution)/shard_map/ppermute | solution.py:1234
  317.0 19.6 %collective-permute-start.16 = (bf16[304,384]{1,0:T(8,128)(2,1)S(1)}, bf16[304,384]{1,0:T(8,128)(2,1)S(1)}, u32[]{:S(2)}, u32[]{:S(2)}) collective-permute-start(bf16[304,384]{1,0:T(8,128)(2,1)S(1)} %get-tuple-element.244), channel_id=1, source_target_pairs={{0,2},{1,3},{2,0},{3,1},{4,6},{5,7},{6,4},{7,5},{8,10},{9,11},{10,... | collective-permute-start | bytes 700424 | tf_op jit(solution)/shard_map/ppermute | solution.py:1234
  319.9 16.7 %collective-permute-start.17 = (bf16[304,384]{1,0:T(8,128)(2,1)S(1)}, bf16[304,384]{1,0:T(8,128)(2,1)S(1)}, u32[]{:S(2)}, u32[]{:S(2)}) collective-permute-start(bf16[304,384]{1,0:T(8,128)(2,1)S(1)} %get-tuple-element.244), channel_id=1, source_target_pairs={{0,3},{1,2},{2,1},{3,0},{4,7},{5,6},{6,5},{7,4},{8,11},{9,10},{10,... | collective-permute-start | bytes 700424 | tf_op jit(solution)/shard_map/ppermute | solution.py:1234
  336.8 9.7 %collective-permute-start.20 = (bf16[608,384]{1,0:T(8,128)(2,1)S(1)}, bf16[608,384]{1,0:T(8,128)(2,1)S(1)}, u32[]{:S(2)}, u32[]{:S(2)}) collective-permute-start(bf16[608,384]{1,0:T(8,128)(2,1)S(1)} %get-tuple-element.234), channel_id=1, source_target_pairs={{0,16},{8,24},{16,0},{24,8},{1,17},{9,25},{17,1},{25,9},{2,18},{10... | collective-permute-start | bytes 1400840 | tf_op jit(solution)/shard_map/ppermute | solution.py:1234
  338.4 13.1 %collective-permute-start.18 = (bf16[608,384]{1,0:T(8,128)(2,1)S(1)}, bf16[608,384]{1,0:T(8,128)(2,1)S(1)}, u32[]{:S(2)}, u32[]{:S(2)}) collective-permute-start(bf16[608,384]{1,0:T(8,128)(2,1)S(1)} %get-tuple-element.235), channel_id=1, source_target_pairs={{0,8},{8,0},{16,24},{24,16},{1,9},{9,1},{17,25},{25,17},{2,10},{10... | collective-permute-start | bytes 1400840 | tf_op jit(solution)/shard_map/ppermute | solution.py:1234
  346.6 24.1 %copy-start.5 = (bf16[1216,384]{1,0:T(8,128)(2,1)}, bf16[1216,384]{1,0:T(8,128)(2,1)S(1)}, u32[]{:S(2)}) copy-start(bf16[1216,384]{1,0:T(8,128)(2,1)S(1)} %pad_maximum_fusion.1.refs_2_) | copy-start | bytes 2801668
  346.6 24.6 %collective-permute-start.21 = (bf16[1216,384]{1,0:T(8,128)(2,1)S(1)}, bf16[1216,384]{1,0:T(8,128)(2,1)S(1)}, u32[]{:S(2)}, u32[]{:S(2)}) collective-permute-start(bf16[1216,384]{1,0:T(8,128)(2,1)S(1)} %pad_maximum_fusion.1.refs_2_), channel_id=1, source_target_pairs={{0,8},{8,0},{16,24},{24,16},{1,9},{9,1},{17,25},{25,17},{2,10},{10... | collective-permute-start | bytes 2801672 | tf_op jit(solution)/shard_map/ppermute | solution.py:1234
  351.5 22.5 %copy-start.6 = (bf16[1216,384]{1,0:T(8,128)(2,1)}, bf16[1216,384]{1,0:T(8,128)(2,1)S(1)}, u32[]{:S(2)}) copy-start(bf16[1216,384]{1,0:T(8,128)(2,1)S(1)} %pad_maximum_fusion.refs_0_) | copy-start | bytes 2801668
  351.6 20.8 %copy-start.2 = (bf16[4,7,72,384]{3,2,1,0:T(8,128)(2,1)S(1)}, bf16[4,7,72,384]{3,2,1,0:T(8,128)(2,1)}, u32[]{:S(2)}) copy-start(bf16[4,7,72,384]{3,2,1,0:T(8,128)(2,1)} %copy-done.1) | copy-start | bytes 4644868
  351.6 19.6 %collective-permute-start.19 = (bf16[1216,384]{1,0:T(8,128)(2,1)S(1)}, bf16[1216,384]{1,0:T(8,128)(2,1)S(1)}, u32[]{:S(2)}, u32[]{:S(2)}) collective-permute-start(bf16[1216,384]{1,0:T(8,128)(2,1)S(1)} %pad_maximum_fusion.refs_0_), channel_id=1, source_target_pairs={{0,16},{8,24},{16,0},{24,8},{1,17},{9,25},{17,1},{25,9},{2,18},{10... | collective-permute-start | bytes 2801672 | tf_op jit(solution)/shard_map/ppermute | solution.py:1234
  351.6 11.0 %collective-permute-start.22 = (bf16[7,72,384]{2,1,0:T(8,128)(2,1)S(1)}, bf16[7,72,384]{2,1,0:T(8,128)(2,1)S(1)}, u32[]{:S(2)}, u32[]{:S(2)}) collective-permute-start(bf16[7,72,384]{2,1,0:T(8,128)(2,1)S(1)} %get-tuple-element.231), channel_id=1, source_target_pairs={{0,1},{1,2},{2,3},{3,0},{4,5},{5,6},{6,7},{7,4},{8,9},{9,10},{10,1... | collective-permute-start | bytes 1161224 | tf_op jit(solution)/shard_map/ppermute | solution.py:1272
  353.8 13.0 %collective-permute-start.23 = (bf16[7,72,384]{2,1,0:T(8,128)(2,1)S(1)}, bf16[7,72,384]{2,1,0:T(8,128)(2,1)S(1)}, u32[]{:S(2)}, u32[]{:S(2)}) collective-permute-start(bf16[7,72,384]{2,1,0:T(8,128)(2,1)S(1)} %get-tuple-element.230), channel_id=1, source_target_pairs={{0,3},{1,0},{2,1},{3,2},{4,7},{5,4},{6,5},{7,6},{8,11},{9,8},{10,9... | collective-permute-start | bytes 1161224 | tf_op jit(solution)/shard_map/ppermute | solution.py:1272
  362.6 4.2 %copy-start.16 = (bf16[7,72,384]{2,1,0:T(8,128)(2,1)}, bf16[7,72,384]{2,1,0:T(8,128)(2,1)S(1)}, u32[]{:S(2)}) copy-start(bf16[7,72,384]{2,1,0:T(8,128)(2,1)S(1)} %collective-permute-done.22.refs_1_) | copy-start | bytes 1161220
  370.7 3.4 copy-start.4
  370.7 5.6 %collective-permute-start.26 = (bf16[1216,384]{1,0:T(8,128)(2,1)S(1)}, bf16[1216,384]{1,0:T(8,128)(2,1)S(1)}, u32[]{:S(2)}, u32[]{:S(2)}) collective-permute-start(bf16[1216,384]{1,0:T(8,128)(2,1)S(1)} %pad_maximum_fusion.1.refs_2_), channel_id=1, source_target_pairs={{0,4},{4,0},{1,5},{5,1},{2,6},{6,2},{3,7},{7,3},{8,12},{12,8},{9,1... | collective-permute-start | bytes 2801672 | tf_op jit(solution)/shard_map/ppermute | solution.py:1234
  370.7 5.6 %collective-permute-start.24 = (bf16[1216,384]{1,0:T(8,128)(2,1)S(1)}, bf16[1216,384]{1,0:T(8,128)(2,1)S(1)}, u32[]{:S(2)}, u32[]{:S(2)}) collective-permute-start(bf16[1216,384]{1,0:T(8,128)(2,1)S(1)} %pad_maximum_fusion.refs_0_), channel_id=1, source_target_pairs={{0,4},{4,0},{1,5},{5,1},{2,6},{6,2},{3,7},{7,3},{8,12},{12,8},{9,1... | collective-permute-start | bytes 2801672 | tf_op jit(solution)/shard_map/ppermute | solution.py:1234
  371.2 5.1 %copy-start.9 = (bf16[1216,384]{1,0:T(8,128)(2,1)}, bf16[1216,384]{1,0:T(8,128)(2,1)S(1)}, u32[]{:S(2)}) copy-start(bf16[1216,384]{1,0:T(8,128)(2,1)S(1)} %collective-permute-done.21.refs_3_) | copy-start | bytes 2801668
  371.2 5.1 %copy-start.10 = (bf16[1216,384]{1,0:T(8,128)(2,1)}, bf16[1216,384]{1,0:T(8,128)(2,1)S(1)}, u32[]{:S(2)}) copy-start(bf16[1216,384]{1,0:T(8,128)(2,1)S(1)} %collective-permute-done.19.refs_1_) | copy-start | bytes 2801668
  371.2 6.0 %collective-permute-start.25 = (bf16[1216,384]{1,0:T(8,128)(2,1)S(1)}, bf16[1216,384]{1,0:T(8,128)(2,1)S(1)}, u32[]{:S(2)}, u32[]{:S(2)}) collective-permute-start(bf16[1216,384]{1,0:T(8,128)(2,1)S(1)} %collective-permute-done.19.refs_1_), channel_id=1, source_target_pairs={{0,4},{4,0},{1,5},{5,1},{2,6},{6,2},{3,7},{7,3},{8,12},{12,8},{9,1... | collective-permute-start | bytes 2801672 | tf_op jit(solution)/shard_map/ppermute | solution.py:1234
  371.3 6.9 %collective-permute-start.27 = (bf16[1216,384]{1,0:T(8,128)(2,1)S(1)}, bf16[1216,384]{1,0:T(8,128)(2,1)}, u32[]{:S(2)}, u32[]{:S(2)}) collective-permute-start(bf16[1216,384]{1,0:T(8,128)(2,1)S(1)} %collective-permute-done.21.refs_3_), channel_id=1, source_target_pairs={{0,4},{4,0},{1,5},{5,1},{2,6},{6,2},{3,7},{7,3},{8,12},{12,8},{9,1... | collective-permute-start | bytes 2801672 | tf_op jit(solution)/shard_map/ppermute | solution.py:1234
  (8 other events, 11.0 us)
where the time goes:
time: 394 us; the launch traced here: 387 us
  Pallas kernels  224 us (57%)
  waiting for transfers between devices  84.9 us (22%)
  starting transfers between devices  48.9 us (12%)
  local copies, waits for them, and re-layouts  18.7 us (5%)
  other arithmetic  8.06 us (2%)
    pallas_call x10, Pallas kernels, call(): pl.pallas_call(body, grid=(steps,), in_specs=[spec(block, index) for _, b...  206 us
    ppermute x25, waiting for transfers between devices, exchange(): return lax.ppermute(part, axis, [(i, i ^ step) for i in range(size)])  31.6 us
    all_to_all x2, waiting for transfers between devices, spread_image(): lax.all_to_all(field, 'rows', 0, 0, axis_index_groups=members, tiled=True)  27.9 us
    ppermute x25, starting transfers between devices, exchange(): return lax.ppermute(part, axis, [(i, i ^ step) for i in range(size)])  26.4 us
    ppermute x3, waiting for transfers between devices, send_tokens(): part = lax.ppermute(part, 'rows', pairs)  25.4 us
    all_to_all x2, starting transfers between devices, spread_image(): lax.all_to_all(field, 'rows', 0, 0, axis_index_groups=members, tiled=True)  10 us
    pallas_call x1, Pallas kernels, assemble(): pl.pallas_call(functools.partial(final_kernel, shares=shares, members=mem...  8.92 us
    unnamed x53, local copies, waits for them, and re-layouts  8.76 us
  transfers between devices with their start and end apart: 31, of which 13 were waited for; matrix products, arithmetic and copies ran while one was open for 5% of the time, Pallas kernels for 30%

commit v1 on v0

--- a/solution.py
+++ b/solution.py
@@ -214,17 +214,26 @@
     out[...] = norm_of(value[...], vec[10:11, :], vec[11:12, :]).astype(BF16)
 
 
+def column_slices(width):
+    return [slice(at, at + 256) for at in range(0, width, 256)]
+
+
 def mlp_body(normed, up_w, up_b, down_w, hidden, slope, keep):
     rows = normed.shape[0]
-    for at in range(0, up_w.shape[1], 256):
-        cols = slice(at, at + 256)
-        pre = dot(normed[...], up_w[:, cols]) + up_b[:, cols]
+    blocks = column_slices(up_w.shape[1])
+
+    def up(cols):
+        return dot(normed[...], up_w[:, cols]) + up_b[:, cols]
+
+    after = up(blocks[0])
+    for n, cols in enumerate(blocks):
+        pre, after = after, up(blocks[n + 1]) if n + 1 < len(blocks) else None
         for row in range(0, rows, 144):
             act, der = gelu_parts(pre[row : row + 144])
             hidden[row : row + 144, cols] = act.astype(BF16)
             slope[row : row + 144, cols] = der.astype(BF16)
         part = dot(hidden[:, cols], down_w[cols, :])
-        if at == 0:
+        if n == 0:
             keep[...] = part
         else:
             keep[...] += part
@@ -264,26 +273,43 @@
 
 def mlp_down_back(rounded, normed, hidden, slope, pre_grad, up_w, down_w, up_g, up_bg, down_g):
     rows = rounded.shape[0]
-    for at in range(0, up_w.shape[1], 256):
-        cols = slice(at, at + 256)
-        hidden_grad = dot_nt(rounded[...], down_w[cols, :])
+    blocks = column_slices(up_w.shape[1])
+
+    def down(cols):
+        return dot_nt(rounded[...], down_w[cols, :])
+
+    def weights(cols):
+        up_g[:, cols] += dot_tn(normed[...], pre_grad[:, cols])
+        down_g[cols, :] += dot_tn(hidden[:, cols], rounded[...])
+
+    after = down(blocks[0])
+    for n, cols in enumerate(blocks):
+        hidden_grad, after = after, down(blocks[n + 1]) if n + 1 < len(blocks) else None
         total = None
         for row in range(0, rows, 144):
             part = hidden_grad[row : row + 144] * slope[row : row + 144, cols].astype(F32)
             pre_grad[row : row + 144, cols] = part.astype(BF16)
             total = fold(part) if total is None else total + fold(part)
         up_bg[:, cols] += total
-        up_g[:, cols] += dot_tn(normed[...], pre_grad[:, cols])
-        down_g[cols, :] += dot_tn(hidden[:, cols], rounded[...])
+        if n:
+            weights(blocks[n - 1])
+    weights(blocks[-1])
 
 
 def mlp_both(normed, cot, up_w, up_b, down_w, hidden, pre_grad, up_g, up_bg, down_g):
     rows = normed.shape[0]
-
-    def block(at):
-        cols = pl.ds(pl.multiple_of(at, 256), 256)
-        pre = dot(normed[...], up_w[:, cols]) + up_b[:, cols]
-        hidden_grad = dot_nt(cot[...], down_w[cols, :])
+    blocks = column_slices(up_w.shape[1])
+
+    def inputs(cols):
+        return dot(normed[...], up_w[:, cols]) + up_b[:, cols], dot_nt(cot[...], down_w[cols, :])
+
+    def weights(cols):
+        up_g[:, cols] += dot_tn(normed[...], pre_grad[:, cols])
+        down_g[cols, :] += dot_tn(hidden[:, cols], cot[...])
+
+    after = inputs(blocks[0])
+    for n, cols in enumerate(blocks):
+        (pre, hidden_grad), after = after, inputs(blocks[n + 1]) if n + 1 < len(blocks) else None
         total = None
         for row in range(0, rows, 144):
             act, der = gelu_parts(pre[row : row + 144])
@@ -292,15 +318,9 @@
             pre_grad[row : row + 144, cols] = part.astype(BF16)
             total = fold(part) if total is None else total + fold(part)
         up_bg[:, cols] += total
-        up_g[:, cols] += dot_tn(normed[...], pre_grad[:, cols])
-        down_g[cols, :] += dot_tn(hidden[:, cols], cot[...])
-
-    def pair(i, carry):
-        block(i * 512)
-        block(i * 512 + 256)
-        return carry
-
-    lax.fori_loop(0, up_w.shape[1] // 512, pair, 0)
+        if n:
+            weights(blocks[n - 1])
+    weights(blocks[-1])
 
 
 def column_blocks(source, chans):
@@ -1023,7 +1043,7 @@
 
 
 def final_kernel(
-    place, *refs, shares, members,
+    core, plane, *refs, shares, members,
 ):
     inputs, outs, rows = refs[:-15], refs[-15:-1], refs[-1]
     (
@@ -1044,16 +1064,16 @@
             mid, late = (plain_reader(*pair) for pair in zip(*halves))
         else:
             pairs = tuple((half[0:2], half[2:4]) for half in halves)
-            mid = reader(pairs, place[1], mid_share, 0, stride, members)
-            late = reader(pairs, place[1], late_share, mid_share, stride, members)
-
-        @pl.when((place[0] == flag) & (layer == 0))
+            mid = reader(pairs, plane[0], mid_share, 0, stride, members)
+            late = reader(pairs, plane[0], late_share, mid_share, stride, members)
+
+        @pl.when((core[0] == flag) & (layer == 0))
         def _():
             put_attention(late, mix_w, out_w)
             put_feed(lambda at, count: mid(feed_rows + 4 * chans + at, count), 0, up_w, down_w)
             rows[...] = late(4 * chans, SMALL_ROWS)
 
-        @pl.when((place[0] == flag) & (layer == 1))
+        @pl.when((core[0] == flag) & (layer == 1))
         def _():
             put_attention(lambda at, count: mid(feed_rows + at, count), mix_w, out_w)
             put_feed(mid, 0, up_w, down_w)
@@ -1086,7 +1106,7 @@
                     at += 1
 
 
-def assemble(place, arrays, shares, members, ff):
+def assemble(core, plane, arrays, shares, members, ff):
     chans = arrays[0].shape[1]
     shapes = [
         (2, chans, 3 * chans), (2, chans, chans), (2, chans, ff), (2, ff, chans),
@@ -1104,13 +1124,13 @@
     ) = pl.pallas_call(
         functools.partial(final_kernel, shares=shares, members=members),
         grid=(2,),
-        in_specs=[pl.BlockSpec(memory_space=pltpu.SMEM)]
+        in_specs=[pl.BlockSpec(memory_space=pltpu.SMEM)] * 2
         + [pl.BlockSpec(x.shape, lambda i: (0, 0), pipeline_mode=pl.Buffered(1)) for x in arrays],
         out_specs=[out_spec(shape) for shape in shapes],
         out_shape=[jax.ShapeDtypeStruct(shape, F32) for shape in shapes],
         scratch_shapes=[pltpu.VMEM((SMALL_ROWS, chans), F32)],
         compiler_params=pltpu.CompilerParams(vmem_limit_bytes=VMEM_LIMIT),
-    )(place, *arrays)
+    )(core, plane, *arrays)
     return (
         conv_w.transpose(2, 0, 1, 3), conv_b, gain, shift, last_shift, mix_w,
         win_b, chan_b, out_w, out_b, up_w, up_b, down_w, down_b,
@@ -1225,7 +1245,8 @@
         jnp.concatenate([window_bias[:chans], jnp.zeros((chans,), BF16), window_bias[chans:]]).astype(F32)[None],
         channel_bias.astype(F32)[None],
     )
-    x0 = spread_image(pad_image(tokens))
+    field, cotangent = lax.optimization_barrier((pad_image(tokens), cotangent))
+    x0 = spread_image(field)
     cot, small, mask, scale = lax.optimization_barrier((pad_image(cotangent), small, mask, scale))
     cot = spread_image(cot).reshape(rows_here * width, chans)
 
@@ -1307,8 +1328,8 @@
         else:
             arrays = [parts[0], others[0], parts[1], others[1]]
     arrays += [exchange(array, "core", 1) for array in arrays]
-    at = jnp.concatenate([core, lax.axis_index("plane").astype(jnp.int32).reshape(1)])
-    return result, tokens_grad.astype(F32), *assemble(at, arrays, shares, members, up_weight.shape[2])
+    plane = lax.axis_index("plane").astype(jnp.int32).reshape(1)
+    return result, tokens_grad.astype(F32), *assemble(core, plane, arrays, shares, members, up_weight.shape[2])
 
 
 def solution(mesh):

time: 394 us -> 386 us (0.980)
  Pallas kernels: 224 us -> 218 us
    pallas_call x10, Pallas kernels: 206 us -> 200 us  [call(): pl.pallas_call(body, grid=(steps,), in_specs=[spec(block, index) for _, b...]
    unnamed x53 -> x55, local copies, waits for them, and re-layouts: 8.76 us -> 8.63 us
  transfers between devices with their start and end apart: 31 -> 31, of which waited for: 13 -> 14; matrix products, arithmetic and copies ran while one was open for 5% -> 5% of each run, Pallas kernels for 30% -> 30%
where the time goes in v1:
time: 386 us; the launch traced here: 381 us
  Pallas kernels  218 us (56%)
  waiting for transfers between devices  85.4 us (22%)
  starting transfers between devices  48.9 us (13%)
  local copies, waits for them, and re-layouts  18.6 us (5%)
  other arithmetic  7.04 us (2%)
    pallas_call x10, Pallas kernels, call(): pl.pallas_call(body, grid=(steps,), in_specs=[spec(block, index) for _, b...  200 us
    ppermute x25, waiting for transfers between devices, exchange(): return lax.ppermute(part, axis, [(i, i ^ step) for i in range(size)])  32 us
    all_to_all x2, waiting for transfers between devices, spread_image(): lax.all_to_all(field, 'rows', 0, 0, axis_index_groups=members, tiled=True)  27.5 us
    ppermute x25, starting transfers between devices, exchange(): return lax.ppermute(part, axis, [(i, i ^ step) for i in range(size)])  26.2 us
    ppermute x3, waiting for transfers between devices, send_tokens(): part = lax.ppermute(part, 'rows', pairs)  25.9 us
    all_to_all x2, starting transfers between devices, spread_image(): lax.all_to_all(field, 'rows', 0, 0, axis_index_groups=members, tiled=True)  10 us
    pallas_call x1, Pallas kernels, assemble(): pl.pallas_call(functools.partial(final_kernel, shares=shares, members=mem...  8.9 us
    unnamed x55, local copies, waits for them, and re-layouts  8.63 us
  transfers between devices with their start and end apart: 31, of which 14 were waited for; matrix products, arithmetic and copies ran while one was open for 5% of the time, Pallas kernels for 30%

profile of v1, /device:TPU:0, one launch (start us, length us, event | category | flops | bytes accessed | tf_op | source)
XLA Modules:
  0.0 380.6 jit_solution(13245260853861299286)
XLA Ops:
  1.4 1.7 copy_select_fusion.1
  4.4 6.4 %all-to-all-start = ((bf16[4,7,72,384]{3,2,1,0:T(8,128)(2,1)}), bf16[4,7,72,384]{3,2,1,0:T(8,128)(2,1)S(1)}, u32[]{:S(2)}, u32[]{:S(2)}) async-start(bf16[4,7,72,384]{3,2,1,0:T(8,128)(2,1)} %pad.9), calls=%async_computation | async-start | bytes 3096576 | tf_op jit(solution)/shard_map/all_to_all | solution.py:1213
  13.2 1.3 pad.10
  15.8 1.5 shard_map.288
  19.7 27.5 %all-to-all-done = bf16[4,7,72,384]{3,2,1,0:T(8,128)(2,1)S(1)} async-done(((bf16[4,7,72,384]{3,2,1,0:T(8,128)(2,1)}), bf16[4,7,72,384]{3,2,1,0:T(8,128)(2,1)S(1)}, u32[]{:S(2)}, u32[]{:S(2)}) %all-to-all-start) | async-done | bytes 1548320 | tf_op jit(solution)/shard_map/all_to_all | solution.py:1213
  47.3 3.6 all-to-all-start.1
  51.6 19.6 %shard_map.289 = (f32[2016,384]{1,0:T(8,128)}, bf16[2560,384]{1,0:T(8,128)(2,1)}, bf16[2560,1152]{1,0:T(8,128)(2,1)}, bf16[2560,384]{1,0:T(8,128)(2,1)}, f32[2016,384]{1,0:T(8,128)}) custom-call(bf16[28,72,384]{2,1,0:T(8,128)(2,1)} %bitcast.20, bf16[28,72,384]{2,1,0:T(8,128)(2,1)} %bitcast.21, bf16[28,72,384]{2,1,0:T(8,128)(2,1)} %bitcast.22, ...), custom_call_target="tpu_custom_call" | custom-call | flops 1 | bytes 72000000 | tf_op jit(solution)/shard_map/pallas_call | solution.py:617
  71.2 23.9 %shard_map.290 = (f32[2016,384]{1,0:T(8,128)}, f32[2016,384]{1,0:T(8,128)}, bf16[2016,384]{1,0:T(8,128)(2,1)}, bf16[2016,1536]{1,0:T(8,128)(2,1)}, bf16[2016,1536]{1,0:T(8,128)(2,1)}) custom-call(f32[2016,384]{1,0:T(8,128)} %get-tuple-element.116.refs_0_.refs_1_.refs_2_.refs_7_, f32[2016,384]{1,0:T(8,128)} %get-tuple-element.116.refs_0_.refs_1_.refs_2_.refs_7_, ...), custom_call_target="tpu_custom_call" | custom-call | flops 1 | bytes 90000000 | tf_op jit(solution)/shard_map/pallas_call | solution.py:617
  95.1 11.2 %shard_map.291 = (f32[2016,384]{1,0:T(8,128)}, bf16[2016,384]{1,0:T(8,128)(2,1)}, bf16[2016,1152]{1,0:T(8,128)(2,1)}, f32[3,128,128]{2,1,0:T(8,128)}) custom-call(f32[2016,384]{1,0:T(8,128)} %get-tuple-element.118.refs_0_.refs_1_.refs_2_.refs_7_, f32[2016,384]{1,0:T(8,128)} %get-tuple-element.118.refs_0_.refs_1_.refs_2_.refs_7_, ...), custom_call_target="tpu_custom_call" | custom-call | flops 1 | bytes 39600000 | tf_op jit(solution)/shard_map/pallas_call | solution.py:617
  106.3 6.6 %shard_map.292 = (bf16[2016,384]{1,0:T(8,128)(2,1)}, f32[2016,384]{1,0:T(8,128)}) custom-call(bf16[2016,1152]{1,0:T(8,128)(2,1)} %get-tuple-element.120.refs_0_.refs_7_.refs_1_, f32[3,128,128]{2,1,0:T(8,128)} %get-tuple-element.121.refs_1_.refs_2_, f32[8,128]{1,0:T(8,128)} %broadcast_in_dim.47.refs_2_.refs_4_, ...), custom_call_target="tpu_custom_call" | custom-call | flops 1 | bytes 25200000 | tf_op jit(solution)/shard_map/pallas_call | solution.py:617
  114.0 35.7 %shard_map.293 = (bf16[2016,384]{1,0:T(8,128)(2,1)}, f32[2016,384]{1,0:T(8,128)}, bf16[3072,384]{1,0:T(8,128)(2,1)}, f32[8,1536]{1,0:T(8,128)}, f32[24,384]{1,0:T(8,128)}) custom-call(f32[2016,384]{1,0:T(8,128)} %get-tuple-element.124.refs_0_.refs_1_.refs_2_.refs_6_, f32[2016,384]{1,0:T(8,128)} %get-tuple-element.124.refs_0_.refs_1_.refs_2_.refs_6_, ...), custom_call_target="tpu_custom_call" | custom-call | flops 1 | bytes 136800000 | tf_op jit(solution)/shard_map/pallas_call | solution.py:617
  149.7 13.0 %shard_map.294 = (f32[2016,384]{1,0:T(8,128)}, bf16[2016,384]{1,0:T(8,128)(2,1)}, f32[3,128,128]{2,1,0:T(8,128)}, bf16[384,384]{1,0:T(8,128)(2,1)}, f32[72,384]{1,0:T(8,128)}, /*index=5*/f32[16,384]{1,0:T(8,128)}) custom-call(f32[2016,384]{1,0:T(8,128)} %get-tuple-element.127.refs_0_.refs_1_.refs_2_, f32[2016,384]{1,0:T(8,128)} %get-tuple-element.127.refs_0_.refs_1_.refs_2_, ...), custom_call_target="tpu_custom_call" | custom-call | flops 1 | bytes 46800000 | tf_op jit(solution)/shard_map/pallas_call | solution.py:617
  162.8 15.6 %shard_map.295 = (f32[2016,384]{1,0:T(8,128)}, bf16[1152,384]{1,0:T(8,128)(2,1)}, f32[8,1152]{1,0:T(8,128)}, f32[16,384]{1,0:T(8,128)}) custom-call(bf16[2016,384]{1,0:T(8,128)(2,1)} %get-tuple-element.129.refs_0_, bf16[2016,1152]{1,0:T(8,128)(2,1)} %get-tuple-element.120.refs_0_.refs_7_.refs_1_, f32[3,128,128]{2,1,0:T(8,128)} %get-tuple-element.121.refs_1_.refs_2_, ...), custom_call_target="tpu_custom_call" | custom-call | flops 1 | bytes 57600000 | tf_op jit(solution)/shard_map/pallas_call | solution.py:617
  178.4 30.6 %shard_map.296 = (f32[2016,384]{1,0:T(8,128)}, bf16[3840,384]{1,0:T(8,128)(2,1)}, bf16[3840,384]{1,0:T(8,128)(2,1)}, f32[8,1536]{1,0:T(8,128)}, f32[72,384]{1,0:T(8,128)}, /*index=5*/f32[32,384]{1,0:T(8,128)}) custom-call(f32[2016,384]{1,0:T(8,128)} %get-tuple-element.133.refs_0_.refs_1_.refs_2_, f32[2016,384]{1,0:T(8,128)} %get-tuple-element.133.refs_0_.refs_1_.refs_2_, ...), custom_call_target="tpu_custom_call" | custom-call | flops 1 | bytes 115200000 | tf_op jit(solution)/shard_map/pallas_call | solution.py:617
  209.0 5.5 %all-to-all-start.2 = ((bf16[4,7,72,384]{3,2,1,0:T(8,128)(2,1)}), bf16[4,7,72,384]{3,2,1,0:T(8,128)(2,1)S(1)}, u32[]{:S(2)}, u32[]{:S(2)}) async-start(bf16[4,7,72,384]{3,2,1,0:T(8,128)(2,1)} %bitcast.4), calls=%async_computation.2 | async-start | bytes 3096576 | tf_op jit(solution)/shard_map/all_to_all | solution.py:1218
  214.7 4.6 %shard_map.297 = (bf16[960,384]{1,0:T(8,128)(2,1)}, bf16[960,384]{1,0:T(8,128)(2,1)}, bf16[960,384]{1,0:T(8,128)(2,1)}, bf16[960,384]{1,0:T(8,128)(2,1)}) custom-call(s32[1]{0:T(128)} %bitcast.5.me.plane, bf16[3840,384]{1,0:T(8,128)(2,1)} %get-tuple-element.141.refs_0_, bf16[3840,384]{1,0:T(8,128)(2,1)} %collective-permute-done.refs_1_), custom_call_target="tpu_custom_call" | custom-call | tf_op jit(solution)/shard_map/pallas_call | solution.py:1157
  219.3 1.5 collective-permute-start.1
  220.8 1.6 collective-permute-start.2
  222.8 33.9 %shard_map.298 = (f32[2016,384]{1,0:T(8,128)}, bf16[1536,384]{1,0:T(8,128)(2,1)}, f32[8,1152]{1,0:T(8,128)}, f32[72,384]{1,0:T(8,128)}, f32[32,384]{1,0:T(8,128)}) custom-call(f32[2016,384]{1,0:T(8,128)} %get-tuple-element.147.refs_0_.refs_1_.refs_2_, f32[2016,384]{1,0:T(8,128)} %get-tuple-element.147.refs_0_.refs_1_.refs_2_, ...), custom_call_target="tpu_custom_call" | custom-call | flops 1 | bytes 122400000 | tf_op jit(solution)/shard_map/pallas_call | solution.py:617
  256.8 2.0 add_convert_fusion.1
  259.5 2.0 collective-permute-start.4
  261.5 2.3 collective-permute-start.5
  265.0 9.8 %shard_map.299 = (bf16[2016,384]{1,0:T(8,128)(2,1)}, bf16[1024,384]{1,0:T(8,128)(2,1)}, bf16[1024,384]{1,0:T(8,128)(2,1)}) custom-call(f32[2016,384]{1,0:T(8,128)} %get-tuple-element.153.refs_0_.refs_1_.refs_2_, f32[2016,384]{1,0:T(8,128)} %get-tuple-element.153.refs_0_.refs_1_.refs_2_, f32[2016,384]{1,0:T(8,128)} %get-tuple-element.153.refs_0_.refs_1_.refs_2_, ...), custom_call_target="tpu_custom_call" | custom-call | flops 1 | bytes 36000000 | tf_op jit(solution)/shard_map/pallas_call | solution.py:617
  274.9 3.0 collective-permute-done.5
  278.0 2.3 dynamic-slice_bitcast_fusion
  280.4 3.4 collective-permute-start.11
  284.1 2.5 collective-permute-start.10
  287.7 14.1 %collective-permute-done.11.refs_2_ = bf16[7,72,384]{2,1,0:T(8,128)(2,1)S(1)} collective-permute-done((bf16[7,72,384]{2,1,0:T(8,128)(2,1)S(1)}, bf16[7,72,384]{2,1,0:T(8,128)(2,1)S(1)}, u32[]{:S(2)}, u32[]{:S(2)}) %collective-permute-start.11) | collective-permute-done | bytes 387104 | tf_op jit(solution)/shard_map/ppermute | solution.py:1293
  302.0 2.0 collective-permute-start.13
  304.0 2.4 collective-permute-start.14
  307.6 2.3 collective-permute-done.14
  310.2 2.9 collective-permute-start.16
  313.1 1.5 collective-permute-start.17
  314.6 5.7 %collective-permute-done.15 = bf16[304,384]{1,0:T(8,128)(2,1)S(1)} collective-permute-done((bf16[304,384]{1,0:T(8,128)(2,1)S(1)}, bf16[304,384]{1,0:T(8,128)(2,1)S(1)}, u32[]{:S(2)}, u32[]{:S(2)}) %collective-permute-start.15) | collective-permute-done | bytes 233504 | tf_op jit(solution)/shard_map/ppermute | solution.py:1255
  320.3 9.5 %collective-permute-done.16 = bf16[304,384]{1,0:T(8,128)(2,1)S(1)} collective-permute-done((bf16[304,384]{1,0:T(8,128)(2,1)S(1)}, bf16[304,384]{1,0:T(8,128)(2,1)S(1)}, u32[]{:S(2)}, u32[]{:S(2)}) %collective-permute-start.16) | collective-permute-done | bytes 233504 | tf_op jit(solution)/shard_map/ppermute | solution.py:1255
  330.0 1.6 collective-permute-start.20
  332.8 7.2 %collective-permute-done.20 = bf16[608,384]{1,0:T(8,128)(2,1)S(1)} collective-permute-done((bf16[608,384]{1,0:T(8,128)(2,1)S(1)}, bf16[608,384]{1,0:T(8,128)(2,1)S(1)}, u32[]{:S(2)}, u32[]{:S(2)}) %collective-permute-start.20) | collective-permute-done | bytes 466976 | tf_op jit(solution)/shard_map/ppermute | solution.py:1255
  340.1 1.8 collective-permute-start.21
  341.9 2.5 collective-permute-done.18
  344.6 2.5 collective-permute-start.22
  347.1 1.4 collective-permute-start.23
  348.4 7.7 %collective-permute-done.22.refs_1_ = bf16[7,72,384]{2,1,0:T(8,128)(2,1)S(1)} collective-permute-done((bf16[7,72,384]{2,1,0:T(8,128)(2,1)S(1)}, bf16[7,72,384]{2,1,0:T(8,128)(2,1)S(1)}, u32[]{:S(2)}, u32[]{:S(2)}) %collective-permute-start.22) | collective-permute-done | bytes 387104 | tf_op jit(solution)/shard_map/ppermute | solution.py:1293
  356.1 4.1 %collective-permute-done.23.refs_3_ = bf16[7,72,384]{2,1,0:T(8,128)(2,1)S(1)} collective-permute-done((bf16[7,72,384]{2,1,0:T(8,128)(2,1)S(1)}, bf16[7,72,384]{2,1,0:T(8,128)(2,1)S(1)}, u32[]{:S(2)}, u32[]{:S(2)}) %collective-permute-start.23) | collective-permute-done | bytes 387104 | tf_op jit(solution)/shard_map/ppermute | solution.py:1293
  361.0 3.1 shard_map.300
  365.2 1.7 copy.42
  366.9 2.2 copy.43
  369.2 1.3 collective-permute-done.25.refs_5_
  371.5 8.9 %shard_map.301 = (f32[2,384,1152]{2,1,0:T(8,128)}, f32[2,384,384]{2,1,0:T(8,128)}, f32[2,384,1536]{2,1,0:T(8,128)}, f32[2,1536,384]{2,1,0:T(8,128)}, f32[3,3,4,3...) custom-call(s32[1]{0:T(128)} %bitcast.6.refs_17_.refs_7_.core, ...), custom_call_target="tpu_custom_call" | custom-call | tf_op jit(solution)/shard_map/pallas_call | solution.py:1124
  (118 shorter events, 19.0 us)
Async XLA Ops:
  4.4 6.5 %copy-start.25 = (s32[4]{0:T(128)S(1)}, s32[4]{0:T(128)}, u32[]{:S(2)}) copy-start(s32[4]{0:T(128)} %param.18) | copy-start | bytes 52
  4.4 8.4 %copy-start.9 = (bf16[4,7,70,384]{3,0,2,1:T(4,128)(2,1)S(1)}, bf16[4,7,70,384]{3,0,2,1:T(4,128)(2,1)}, u32[]{:S(2)}) copy-start(bf16[4,7,70,384]{3,0,2,1:T(4,128)(2,1)} %param.32) | copy-start | bytes 4515844
  4.4 42.9 %all-to-all-start = ((bf16[4,7,72,384]{3,2,1,0:T(8,128)(2,1)}), bf16[4,7,72,384]{3,2,1,0:T(8,128)(2,1)S(1)}, u32[]{:S(2)}, u32[]{:S(2)}) async-start(bf16[4,7,72,384]{3,2,1,0:T(8,128)(2,1)} %pad.9), calls=%async_computation | async-start | bytes 3096576 | tf_op jit(solution)/shard_map/all_to_all | solution.py:1213
  47.3 4.3 %copy-start = (bf16[4,7,72,384]{3,2,1,0:T(8,128)(2,1)}, bf16[4,7,72,384]{3,2,1,0:T(8,128)(2,1)S(1)}, u32[]{:S(2)}) copy-start(bf16[4,7,72,384]{3,2,1,0:T(8,128)(2,1)S(1)} %all-to-all-done) | copy-start | bytes 4644868
  47.3 65.6 %all-to-all-start.1 = ((bf16[4,7,72,384]{3,2,1,0:T(8,128)(2,1)}), bf16[4,7,72,384]{3,2,1,0:T(8,128)(2,1)S(1)}, u32[]{:S(2)}, u32[]{:S(2)}) async-start(bf16[4,7,72,384]{3,2,1,0:T(8,128)(2,1)} %pad.10), calls=%async_computation.1 | async-start | bytes 3096576 | tf_op jit(solution)/shard_map/all_to_all | solution.py:1213
  208.9 5.8 %collective-permute-start = (bf16[3840,384]{1,0:T(8,128)(2,1)}, bf16[3840,384]{1,0:T(8,128)(2,1)}, u32[]{:S(2)}, u32[]{:S(2)}) collective-permute-start(bf16[3840,384]{1,0:T(8,128)(2,1)} %get-tuple-element.142), channel_id=1, source_target_pairs={{0,4},{4,0},{1,5},{5,1},{2,6},{6,2},{3,7},{7,3},{8,12},{12,8},{9,1... | collective-permute-start | bytes 8847368 | tf_op jit(solution)/shard_map/ppermute | solution.py:1255
  209.0 54.9 %all-to-all-start.2 = ((bf16[4,7,72,384]{3,2,1,0:T(8,128)(2,1)}), bf16[4,7,72,384]{3,2,1,0:T(8,128)(2,1)S(1)}, u32[]{:S(2)}, u32[]{:S(2)}) async-start(bf16[4,7,72,384]{3,2,1,0:T(8,128)(2,1)} %bitcast.4), calls=%async_computation.2 | async-start | bytes 3096576 | tf_op jit(solution)/shard_map/all_to_all | solution.py:1218
  219.3 37.4 %collective-permute-start.1 = (bf16[960,384]{1,0:T(8,128)(2,1)}, bf16[960,384]{1,0:T(8,128)(2,1)S(1)}, u32[]{:S(2)}, u32[]{:S(2)}) collective-permute-start(bf16[960,384]{1,0:T(8,128)(2,1)} %get-tuple-element.144), channel_id=1, source_target_pairs={{0,8},{8,0},{16,24},{24,16},{1,9},{9,1},{17,25},{25,17},{2,10},{10... | collective-permute-start | bytes 2211848 | tf_op jit(solution)/shard_map/ppermute | solution.py:1255
  220.8 36.0 %collective-permute-start.2 = (bf16[960,384]{1,0:T(8,128)(2,1)}, bf16[960,384]{1,0:T(8,128)(2,1)}, u32[]{:S(2)}, u32[]{:S(2)}) collective-permute-start(bf16[960,384]{1,0:T(8,128)(2,1)} %get-tuple-element.145), channel_id=1, source_target_pairs={{0,16},{8,24},{16,0},{24,8},{1,17},{9,25},{17,1},{25,9},{2,18},{10... | collective-permute-start | bytes 2211848 | tf_op jit(solution)/shard_map/ppermute | solution.py:1255
  222.4 34.4 %collective-permute-start.3 = (bf16[960,384]{1,0:T(8,128)(2,1)}, bf16[960,384]{1,0:T(8,128)(2,1)}, u32[]{:S(2)}, u32[]{:S(2)}) collective-permute-start(bf16[960,384]{1,0:T(8,128)(2,1)} %get-tuple-element.146), channel_id=1, source_target_pairs={{0,24},{8,16},{16,8},{24,0},{1,25},{9,17},{17,9},{25,1},{2,26},{10... | collective-permute-start | bytes 2211848 | tf_op jit(solution)/shard_map/ppermute | solution.py:1255
  222.8 34.0 %copy-start.7 = (bf16[960,384]{1,0:T(8,128)(2,1)S(1)}, bf16[960,384]{1,0:T(8,128)(2,1)}, u32[]{:S(2)}) copy-start(bf16[960,384]{1,0:T(8,128)(2,1)} %get-tuple-element.167.refs_22_) | copy-start | bytes 2211844
  259.5 15.4 %collective-permute-start.4 = (bf16[240,384]{1,0:T(8,128)(2,1)}, bf16[240,384]{1,0:T(8,128)(2,1)S(1)}, u32[]{:S(2)}, u32[]{:S(2)}) collective-permute-start(bf16[240,384]{1,0:T(8,128)(2,1)} %get-tuple-element.246), channel_id=1, source_target_pairs={{0,1},{1,0},{2,3},{3,2},{4,5},{5,4},{6,7},{7,6},{8,9},{9,8},{10,11... | collective-permute-start | bytes 552968 | tf_op jit(solution)/shard_map/ppermute | solution.py:1255
  261.5 16.4 %collective-permute-start.5 = (bf16[240,384]{1,0:T(8,128)(2,1)S(1)}, bf16[240,384]{1,0:T(8,128)(2,1)S(1)}, u32[]{:S(2)}, u32[]{:S(2)}) collective-permute-start(bf16[240,384]{1,0:T(8,128)(2,1)S(1)} %get-tuple-element.245), channel_id=1, source_target_pairs={{0,2},{1,3},{2,0},{3,1},{4,6},{5,7},{6,4},{7,5},{8,10},{9,11},{10,... | collective-permute-start | bytes 552968 | tf_op jit(solution)/shard_map/ppermute | solution.py:1255
  263.9 14.1 %collective-permute-start.6 = (bf16[240,384]{1,0:T(8,128)(2,1)S(1)}, bf16[240,384]{1,0:T(8,128)(2,1)}, u32[]{:S(2)}, u32[]{:S(2)}) collective-permute-start(bf16[240,384]{1,0:T(8,128)(2,1)S(1)} %get-tuple-element.244), channel_id=1, source_target_pairs={{0,3},{1,2},{2,1},{3,0},{4,7},{5,6},{6,5},{7,4},{8,11},{9,10},{10,... | collective-permute-start | bytes 552968 | tf_op jit(solution)/shard_map/ppermute | solution.py:1255
  274.9 5.5 %copy-start.19 = (bf16[240,384]{1,0:T(8,128)(2,1)}, bf16[240,384]{1,0:T(8,128)(2,1)S(1)}, u32[]{:S(2)}) copy-start(bf16[240,384]{1,0:T(8,128)(2,1)S(1)} %collective-permute-done.4) | copy-start | bytes 552964
  277.9 2.4 copy-start.21
  277.9 5.9 %collective-permute-start.7 = (bf16[1024,384]{1,0:T(8,128)(2,1)}, bf16[1024,384]{1,0:T(8,128)(2,1)S(1)}, u32[]{:S(2)}, u32[]{:S(2)}) collective-permute-start(bf16[1024,384]{1,0:T(8,128)(2,1)} %get-tuple-element.178), channel_id=1, source_target_pairs={{0,4},{4,0},{1,5},{5,1},{2,6},{6,2},{3,7},{7,3},{8,12},{12,8},{9,1... | collective-permute-start | bytes 2359304 | tf_op jit(solution)/shard_map/ppermute | solution.py:1255
  278.0 5.8 %copy-start.15 = (bf16[1024,384]{1,0:T(8,128)(2,1)S(1)}, bf16[1024,384]{1,0:T(8,128)(2,1)}, u32[]{:S(2)}) copy-start(bf16[1024,384]{1,0:T(8,128)(2,1)} %get-tuple-element.177) | copy-start | bytes 2359300
  280.4 21.4 %collective-permute-start.11 = (bf16[7,72,384]{2,1,0:T(8,128)(2,1)S(1)}, bf16[7,72,384]{2,1,0:T(8,128)(2,1)S(1)}, u32[]{:S(2)}, u32[]{:S(2)}) collective-permute-start(bf16[7,72,384]{2,1,0:T(8,128)(2,1)S(1)} %get-tuple-element.237), channel_id=1, source_target_pairs={{0,2},{1,3},{2,0},{3,1},{4,6},{5,7},{6,4},{7,5},{8,10},{9,11},{10,... | collective-permute-start | bytes 1161224 | tf_op jit(solution)/shard_map/ppermute | solution.py:1293
  284.0 22.4 %copy-start.20 = (bf16[240,384]{1,0:T(8,128)(2,1)S(1)}, bf16[240,384]{1,0:T(8,128)(2,1)}, u32[]{:S(2)}) copy-start(bf16[240,384]{1,0:T(8,128)(2,1)} %copy-done.19) | copy-start | bytes 552964
  284.1 17.6 %collective-permute-start.10 = (bf16[256,384]{1,0:T(8,128)(2,1)S(1)}, bf16[256,384]{1,0:T(8,128)(2,1)S(1)}, u32[]{:S(2)}, u32[]{:S(2)}) collective-permute-start(bf16[256,384]{1,0:T(8,128)(2,1)S(1)} %get-tuple-element.240), channel_id=1, source_target_pairs={{0,24},{8,16},{16,8},{24,0},{1,25},{9,17},{17,9},{25,1},{2,26},{10... | collective-permute-start | bytes 589832 | tf_op jit(solution)/shard_map/ppermute | solution.py:1255
  286.6 15.1 %collective-permute-start.8 = (bf16[256,384]{1,0:T(8,128)(2,1)S(1)}, bf16[256,384]{1,0:T(8,128)(2,1)S(1)}, u32[]{:S(2)}, u32[]{:S(2)}) collective-permute-start(bf16[256,384]{1,0:T(8,128)(2,1)S(1)} %get-tuple-element.242), channel_id=1, source_target_pairs={{0,8},{8,0},{16,24},{24,16},{1,9},{9,1},{17,25},{25,17},{2,10},{10... | collective-permute-start | bytes 589832 | tf_op jit(solution)/shard_map/ppermute | solution.py:1255
  287.2 14.6 %collective-permute-start.9 = (bf16[256,384]{1,0:T(8,128)(2,1)S(1)}, bf16[256,384]{1,0:T(8,128)(2,1)S(1)}, u32[]{:S(2)}, u32[]{:S(2)}) collective-permute-start(bf16[256,384]{1,0:T(8,128)(2,1)S(1)} %get-tuple-element.241), channel_id=1, source_target_pairs={{0,16},{8,24},{16,0},{24,8},{1,17},{9,25},{17,1},{25,9},{2,18},{10... | collective-permute-start | bytes 589832 | tf_op jit(solution)/shard_map/ppermute | solution.py:1255
  301.7 8.3 %copy-start.16 = (bf16[7,72,384]{2,1,0:T(8,128)(2,1)}, bf16[7,72,384]{2,1,0:T(8,128)(2,1)S(1)}, u32[]{:S(2)}) copy-start(bf16[7,72,384]{2,1,0:T(8,128)(2,1)S(1)} %collective-permute-done.11.refs_2_) | copy-start | bytes 1161220
  301.9 5.6 %collective-permute-start.12 = (bf16[64,384]{1,0:T(8,128)(2,1)S(1)}, bf16[64,384]{1,0:T(8,128)(2,1)S(1)}, u32[]{:S(2)}, u32[]{:S(2)}) collective-permute-start(bf16[64,384]{1,0:T(8,128)(2,1)S(1)} %get-tuple-element.250), channel_id=1, source_target_pairs={{0,1},{1,0},{2,3},{3,2},{4,5},{5,4},{6,7},{7,6},{8,9},{9,8},{10,11... | collective-permute-start | bytes 147464 | tf_op jit(solution)/shard_map/ppermute | solution.py:1255
  302.0 5.6 %collective-permute-start.13 = (bf16[64,384]{1,0:T(8,128)(2,1)S(1)}, bf16[64,384]{1,0:T(8,128)(2,1)S(1)}, u32[]{:S(2)}, u32[]{:S(2)}) collective-permute-start(bf16[64,384]{1,0:T(8,128)(2,1)S(1)} %get-tuple-element.252), channel_id=1, source_target_pairs={{0,2},{1,3},{2,0},{3,1},{4,6},{5,7},{6,4},{7,5},{8,10},{9,11},{10,... | collective-permute-start | bytes 147464 | tf_op jit(solution)/shard_map/ppermute | solution.py:1255
  304.0 5.9 %collective-permute-start.14 = (bf16[64,384]{1,0:T(8,128)(2,1)S(1)}, bf16[64,384]{1,0:T(8,128)(2,1)S(1)}, u32[]{:S(2)}, u32[]{:S(2)}) collective-permute-start(bf16[64,384]{1,0:T(8,128)(2,1)S(1)} %get-tuple-element.251), channel_id=1, source_target_pairs={{0,3},{1,2},{2,1},{3,0},{4,7},{5,6},{6,5},{7,4},{8,11},{9,10},{10,... | collective-permute-start | bytes 147464 | tf_op jit(solution)/shard_map/ppermute | solution.py:1255
  310.1 10.1 %collective-permute-start.15 = (bf16[304,384]{1,0:T(8,128)(2,1)S(1)}, bf16[304,384]{1,0:T(8,128)(2,1)S(1)}, u32[]{:S(2)}, u32[]{:S(2)}) collective-permute-start(bf16[304,384]{1,0:T(8,128)(2,1)S(1)} %get-tuple-element.248), channel_id=1, source_target_pairs={{0,1},{1,0},{2,3},{3,2},{4,5},{5,4},{6,7},{7,6},{8,9},{9,8},{10,11... | collective-permute-start | bytes 700424 | tf_op jit(solution)/shard_map/ppermute | solution.py:1255
  310.2 19.6 %collective-permute-start.16 = (bf16[304,384]{1,0:T(8,128)(2,1)S(1)}, bf16[304,384]{1,0:T(8,128)(2,1)S(1)}, u32[]{:S(2)}, u32[]{:S(2)}) collective-permute-start(bf16[304,384]{1,0:T(8,128)(2,1)S(1)} %get-tuple-element.248), channel_id=1, source_target_pairs={{0,2},{1,3},{2,0},{3,1},{4,6},{5,7},{6,4},{7,5},{8,10},{9,11},{10,... | collective-permute-start | bytes 700424 | tf_op jit(solution)/shard_map/ppermute | solution.py:1255
  313.1 16.7 %collective-permute-start.17 = (bf16[304,384]{1,0:T(8,128)(2,1)S(1)}, bf16[304,384]{1,0:T(8,128)(2,1)S(1)}, u32[]{:S(2)}, u32[]{:S(2)}) collective-permute-start(bf16[304,384]{1,0:T(8,128)(2,1)S(1)} %get-tuple-element.248), channel_id=1, source_target_pairs={{0,3},{1,2},{2,1},{3,0},{4,7},{5,6},{6,5},{7,4},{8,11},{9,10},{10,... | collective-permute-start | bytes 700424 | tf_op jit(solution)/shard_map/ppermute | solution.py:1255
  330.0 10.0 %collective-permute-start.20 = (bf16[608,384]{1,0:T(8,128)(2,1)S(1)}, bf16[608,384]{1,0:T(8,128)(2,1)S(1)}, u32[]{:S(2)}, u32[]{:S(2)}) collective-permute-start(bf16[608,384]{1,0:T(8,128)(2,1)S(1)} %get-tuple-element.238), channel_id=1, source_target_pairs={{0,16},{8,24},{16,0},{24,8},{1,17},{9,25},{17,1},{25,9},{2,18},{10... | collective-permute-start | bytes 1400840 | tf_op jit(solution)/shard_map/ppermute | solution.py:1255
  331.6 12.8 %collective-permute-start.18 = (bf16[608,384]{1,0:T(8,128)(2,1)S(1)}, bf16[608,384]{1,0:T(8,128)(2,1)S(1)}, u32[]{:S(2)}, u32[]{:S(2)}) collective-permute-start(bf16[608,384]{1,0:T(8,128)(2,1)S(1)} %get-tuple-element.239), channel_id=1, source_target_pairs={{0,8},{8,0},{16,24},{24,16},{1,9},{9,1},{17,25},{25,17},{2,10},{10... | collective-permute-start | bytes 1400840 | tf_op jit(solution)/shard_map/ppermute | solution.py:1255
  340.0 24.0 %copy-start.5 = (bf16[1216,384]{1,0:T(8,128)(2,1)}, bf16[1216,384]{1,0:T(8,128)(2,1)S(1)}, u32[]{:S(2)}) copy-start(bf16[1216,384]{1,0:T(8,128)(2,1)S(1)} %pad_maximum_fusion.1.refs_2_) | copy-start | bytes 2801668
  340.1 24.5 %collective-permute-start.21 = (bf16[1216,384]{1,0:T(8,128)(2,1)S(1)}, bf16[1216,384]{1,0:T(8,128)(2,1)S(1)}, u32[]{:S(2)}, u32[]{:S(2)}) collective-permute-start(bf16[1216,384]{1,0:T(8,128)(2,1)S(1)} %pad_maximum_fusion.1.refs_2_), channel_id=1, source_target_pairs={{0,8},{8,0},{16,24},{24,16},{1,9},{9,1},{17,25},{25,17},{2,10},{10... | collective-permute-start | bytes 2801672 | tf_op jit(solution)/shard_map/ppermute | solution.py:1255
  344.5 22.4 %copy-start.6 = (bf16[1216,384]{1,0:T(8,128)(2,1)}, bf16[1216,384]{1,0:T(8,128)(2,1)S(1)}, u32[]{:S(2)}) copy-start(bf16[1216,384]{1,0:T(8,128)(2,1)S(1)} %pad_maximum_fusion.refs_0_) | copy-start | bytes 2801668
  344.5 20.7 %copy-start.2 = (bf16[4,7,72,384]{3,2,1,0:T(8,128)(2,1)S(1)}, bf16[4,7,72,384]{3,2,1,0:T(8,128)(2,1)}, u32[]{:S(2)}) copy-start(bf16[4,7,72,384]{3,2,1,0:T(8,128)(2,1)} %copy-done.1) | copy-start | bytes 4644868
  344.5 20.1 %collective-permute-start.19 = (bf16[1216,384]{1,0:T(8,128)(2,1)S(1)}, bf16[1216,384]{1,0:T(8,128)(2,1)S(1)}, u32[]{:S(2)}, u32[]{:S(2)}) collective-permute-start(bf16[1216,384]{1,0:T(8,128)(2,1)S(1)} %pad_maximum_fusion.refs_0_), channel_id=1, source_target_pairs={{0,16},{8,24},{16,0},{24,8},{1,17},{9,25},{17,1},{25,9},{2,18},{10... | collective-permute-start | bytes 2801672 | tf_op jit(solution)/shard_map/ppermute | solution.py:1255
  344.6 11.5 %collective-permute-start.22 = (bf16[7,72,384]{2,1,0:T(8,128)(2,1)S(1)}, bf16[7,72,384]{2,1,0:T(8,128)(2,1)S(1)}, u32[]{:S(2)}, u32[]{:S(2)}) collective-permute-start(bf16[7,72,384]{2,1,0:T(8,128)(2,1)S(1)} %get-tuple-element.235), channel_id=1, source_target_pairs={{0,1},{1,2},{2,3},{3,0},{4,5},{5,6},{6,7},{7,4},{8,9},{9,10},{10,1... | collective-permute-start | bytes 1161224 | tf_op jit(solution)/shard_map/ppermute | solution.py:1293
  347.1 13.2 %collective-permute-start.23 = (bf16[7,72,384]{2,1,0:T(8,128)(2,1)S(1)}, bf16[7,72,384]{2,1,0:T(8,128)(2,1)S(1)}, u32[]{:S(2)}, u32[]{:S(2)}) collective-permute-start(bf16[7,72,384]{2,1,0:T(8,128)(2,1)S(1)} %get-tuple-element.234), channel_id=1, source_target_pairs={{0,3},{1,0},{2,1},{3,2},{4,7},{5,4},{6,5},{7,6},{8,11},{9,8},{10,9... | collective-permute-start | bytes 1161224 | tf_op jit(solution)/shard_map/ppermute | solution.py:1293
  356.1 4.1 %copy-start.17 = (bf16[7,72,384]{2,1,0:T(8,128)(2,1)}, bf16[7,72,384]{2,1,0:T(8,128)(2,1)S(1)}, u32[]{:S(2)}) copy-start(bf16[7,72,384]{2,1,0:T(8,128)(2,1)S(1)} %collective-permute-done.22.refs_1_) | copy-start | bytes 1161220
  364.1 2.8 copy-start.4
  364.1 5.0 %collective-permute-start.26 = (bf16[1216,384]{1,0:T(8,128)(2,1)S(1)}, bf16[1216,384]{1,0:T(8,128)(2,1)S(1)}, u32[]{:S(2)}, u32[]{:S(2)}) collective-permute-start(bf16[1216,384]{1,0:T(8,128)(2,1)S(1)} %pad_maximum_fusion.1.refs_2_), channel_id=1, source_target_pairs={{0,4},{4,0},{1,5},{5,1},{2,6},{6,2},{3,7},{7,3},{8,12},{12,8},{9,1... | collective-permute-start | bytes 2801672 | tf_op jit(solution)/shard_map/ppermute | solution.py:1255
  364.1 5.2 %collective-permute-start.24 = (bf16[1216,384]{1,0:T(8,128)(2,1)S(1)}, bf16[1216,384]{1,0:T(8,128)(2,1)S(1)}, u32[]{:S(2)}, u32[]{:S(2)}) collective-permute-start(bf16[1216,384]{1,0:T(8,128)(2,1)S(1)} %pad_maximum_fusion.refs_0_), channel_id=1, source_target_pairs={{0,4},{4,0},{1,5},{5,1},{2,6},{6,2},{3,7},{7,3},{8,12},{12,8},{9,1... | collective-permute-start | bytes 2801672 | tf_op jit(solution)/shard_map/ppermute | solution.py:1255
  364.6 4.5 %copy-start.10 = (bf16[1216,384]{1,0:T(8,128)(2,1)}, bf16[1216,384]{1,0:T(8,128)(2,1)S(1)}, u32[]{:S(2)}) copy-start(bf16[1216,384]{1,0:T(8,128)(2,1)S(1)} %collective-permute-done.21.refs_3_) | copy-start | bytes 2801668
  364.6 4.5 %copy-start.11 = (bf16[1216,384]{1,0:T(8,128)(2,1)}, bf16[1216,384]{1,0:T(8,128)(2,1)S(1)}, u32[]{:S(2)}) copy-start(bf16[1216,384]{1,0:T(8,128)(2,1)S(1)} %collective-permute-done.19.refs_1_) | copy-start | bytes 2801668
  364.6 6.0 %collective-permute-start.25 = (bf16[1216,384]{1,0:T(8,128)(2,1)S(1)}, bf16[1216,384]{1,0:T(8,128)(2,1)S(1)}, u32[]{:S(2)}, u32[]{:S(2)}) collective-permute-start(bf16[1216,384]{1,0:T(8,128)(2,1)S(1)} %collective-permute-done.19.refs_1_), channel_id=1, source_target_pairs={{0,4},{4,0},{1,5},{5,1},{2,6},{6,2},{3,7},{7,3},{8,12},{12,8},{9,1... | collective-permute-start | bytes 2801672 | tf_op jit(solution)/shard_map/ppermute | solution.py:1255
  364.7 6.8 %collective-permute-start.27 = (bf16[1216,384]{1,0:T(8,128)(2,1)S(1)}, bf16[1216,384]{1,0:T(8,128)(2,1)}, u32[]{:S(2)}, u32[]{:S(2)}) collective-permute-start(bf16[1216,384]{1,0:T(8,128)(2,1)S(1)} %collective-permute-done.21.refs_3_), channel_id=1, source_target_pairs={{0,4},{4,0},{1,5},{5,1},{2,6},{6,2},{3,7},{7,3},{8,12},{12,8},{9,1... | collective-permute-start | bytes 2801672 | tf_op jit(solution)/shard_map/ppermute | solution.py:1255
  369.1 2.4 copy-start.12
  (9 other events, 12.1 us)
